TPU v7x, 256 devices: a whole 4x4x8 slice. The times are simulated.
256 devices in a mesh: gen: 32 (over y, x, core), beam: 8 (over z).
Axes of the slice: x: 4, y: 4, z: 8, core: 2. Of those that a mesh axis runs over, the one named last changes fastest.
Arguments:
- gen_showers: bfloat16 [32768, 256], P('gen'), may hold values from -12 to 12
- beam_showers: bfloat16 [16384, 256], P('beam'), may hold values from -6 to 6
- embed_weight: bfloat16 [256, 128], replicated, may hold values from -0.375 to 0.375
- eps_roster: float32 [4], replicated, may hold values from 0.04 to 0.08
Outputs:
- gen_potential: float32 [32768], P('gen')
- beam_potential: float32 [16384], P('beam')
- weight_grad: float32 [256, 128], replicated
All inputs are finite; a program needn't handle non-finite values.
Results may differ from a plain program's by a relative error of at most 0.03.
Values sent between devices are 32-bit elements; how exact they have to be, the bound alone decides.
No kernel may reach another device: no remote copies, remote signals or barrier semaphores. Data moves between devices by JAX's collectives and lax.ppermute only.
A program may use at most 64 MiB of HBM per device.

v0:
```python
import math

import jax
import jax.numpy as jnp
from jax import lax
from jax.sharding import PartitionSpec as P

SWEEPS = 4


def embed(showers, weight):
    act = jnp.tanh(jnp.dot(showers, weight, preferred_element_type=jnp.float32))
    return (act, act.astype(jnp.bfloat16))


def tile_cost(gen_emb, beam_emb, gen_sq, beam_sq):
    cross = lax.dot_general(
        gen_emb, beam_emb, (((1,), (1,)), ((), ())), preferred_element_type=jnp.float32
    )
    return gen_sq[:, None] + beam_sq[None, :] - 2.0 * cross


def row_lse(scores):
    top = lax.pmax(jnp.max(scores, axis=1), "beam")
    total = lax.psum(jnp.sum(jnp.exp(scores - top[:, None]), axis=1), "beam")
    return top + jnp.log(total)


def col_lse(scores):
    top = lax.pmax(jnp.max(scores, axis=0), "gen")
    total = lax.psum(jnp.sum(jnp.exp(scores - top[None, :]), axis=0), "gen")
    return top + jnp.log(total)


def transpose_dot(left, right):
    return lax.dot_general(
        left.astype(jnp.float32),
        right,
        (((0,), (0,)), ((), ())),
        precision=lax.Precision.HIGHEST,
        preferred_element_type=jnp.float32,
    )


def on_device(gen_showers, beam_showers, embed_weight, eps_roster):
    gen_act, gen_emb = embed(gen_showers, embed_weight)
    beam_act, beam_emb = embed(beam_showers, embed_weight)
    gen_float = gen_emb.astype(jnp.float32)
    beam_float = beam_emb.astype(jnp.float32)
    gen_sq = jnp.sum(gen_float * gen_float, axis=1)
    beam_sq = jnp.sum(beam_float * beam_float, axis=1)
    rows = gen_emb.shape[0]
    columns = beam_emb.shape[0]
    log_beam = math.log(columns * lax.axis_size("beam"))
    log_gen = math.log(rows * lax.axis_size("gen"))
    beam_pot = jnp.zeros((columns,), jnp.float32)
    gen_pot = jnp.zeros((rows,), jnp.float32)
    for sweep in range(SWEEPS):
        temper = eps_roster[sweep]
        cost = tile_cost(gen_emb, beam_emb, gen_sq, beam_sq)
        gen_pot = temper * (log_beam - row_lse((beam_pot[None, :] - cost) / temper))
        cost = tile_cost(gen_emb, beam_emb, gen_sq, beam_sq)
        beam_pot = temper * (log_gen - col_lse((gen_pot[:, None] - cost) / temper))
    last = eps_roster[SWEEPS - 1]
    cost = tile_cost(gen_emb, beam_emb, gen_sq, beam_sq)
    mass = jnp.exp((gen_pot[:, None] + beam_pot[None, :] - cost) / last - log_beam)
    plan = mass.astype(jnp.bfloat16)
    gen_count = rows // lax.axis_size("beam")
    part = plan
    row_mass = jnp.sum(mass, axis=1)
    own = gen_float
    moved = jnp.dot(part, beam_emb, preferred_element_type=jnp.float32)
    grad_gen = lax.psum_scatter(
        2.0 * (row_mass[:, None] * own - moved), "beam", scatter_dimension=0, tiled=True
    )
    gen_start = lax.axis_index("beam") * gen_count
    act_rows = lax.dynamic_slice_in_dim(gen_act, gen_start, gen_count, 0)
    shower_rows = lax.dynamic_slice_in_dim(gen_showers, gen_start, gen_count, 0)
    beam_count = columns // lax.axis_size("gen")
    part = plan
    col_mass = jnp.sum(mass, axis=0)
    own = beam_float
    moved = lax.dot_general(
        part, gen_emb, (((0,), (0,)), ((), ())), preferred_element_type=jnp.float32
    )
    grad_beam = lax.psum_scatter(
        2.0 * (col_mass[:, None] * own - moved), "gen", scatter_dimension=0, tiled=True
    )
    beam_start = lax.axis_index("gen") * beam_count
    act_cols = lax.dynamic_slice_in_dim(beam_act, beam_start, beam_count, 0)
    shower_cols = lax.dynamic_slice_in_dim(beam_showers, beam_start, beam_count, 0)
    partial_grad = transpose_dot(shower_rows, grad_gen * (1.0 - act_rows * act_rows))
    partial_grad = partial_grad + transpose_dot(
        shower_cols, grad_beam * (1.0 - act_cols * act_cols)
    )
    weight_grad = lax.psum(partial_grad, ("gen", "beam"))
    return (gen_pot, beam_pot, weight_grad)


def solution(mesh):
    in_specs = (P("gen", None), P("beam", None), P(), P())
    out_specs = (P("gen"), P("beam"), P())
    return jax.shard_map(
        on_device, mesh=mesh, in_specs=in_specs, out_specs=out_specs, check_vma=False
    )
```

profile of v0, /device:TPU:1, one launch (start us, length us, event | category | flops | bytes accessed | tf_op | source)
XLA Modules:
  0.0 1114.3 jit_solution(14821040143072383777)
XLA Ops:
  11.4 5.3 fusion
  16.7 17.3 %pmax.56 = f32[1024]{0:T(1024)S(1)} all-reduce(f32[1024]{0:T(1024)S(1)} %get-tuple-element.16), channel_id=1, replica_groups=mesh['gen'=32,'beam'=8] {'beam'}, use_global_device_ids=true, to_apply=%region_3.0 | all-reduce | flops 1024 | bytes 8192 | tf_op jit(solution)/shard_map/pmax | solution.py:24
  34.0 5.1 exponential_reduce_fusion.7
  39.1 10.8 psum.63
  55.2 70.9 %pmax.57 = f32[2048]{0:T(1024)S(1)} all-reduce(f32[2048]{0:T(1024)S(1)} %fusion.15), channel_id=1, replica_groups=mesh['gen'=32,'beam'=8] {'gen'}, use_global_device_ids=true, to_apply=%region_7.0 | all-reduce | flops 2048 | bytes 16384 | tf_op jit(solution)/shard_map/pmax | solution.py:30
  126.1 5.2 exponential_reduce_fusion.6
  131.3 63.4 %psum.64 = f32[2048]{0:T(1024)S(1)} all-reduce(f32[2048]{0:T(1024)S(1)} %exponential_reduce_fusion.6), channel_id=1, replica_groups=mesh['gen'=32,'beam'=8] {'gen'}, use_global_device_ids=true, to_apply=%region_9.0 | all-reduce | flops 2048 | bytes 16384 | tf_op jit(solution)/shard_map/psum | solution.py:31
  195.4 4.8 fusion.1
  200.2 12.4 %pmax.58 = f32[1024]{0:T(1024)S(1)} all-reduce(f32[1024]{0:T(1024)S(1)} %fusion.1), channel_id=1, replica_groups=mesh['gen'=32,'beam'=8] {'beam'}, use_global_device_ids=true, to_apply=%region_11.0 | all-reduce | flops 1024 | bytes 8192 | tf_op jit(solution)/shard_map/pmax | solution.py:24
  212.6 5.1 exponential_reduce_fusion.5
  217.7 10.7 psum.65
  233.6 71.0 %pmax.59 = f32[2048]{0:T(1024)S(1)} all-reduce(f32[2048]{0:T(1024)S(1)} %fusion.16), channel_id=1, replica_groups=mesh['gen'=32,'beam'=8] {'gen'}, use_global_device_ids=true, to_apply=%region_15.0 | all-reduce | flops 2048 | bytes 16384 | tf_op jit(solution)/shard_map/pmax | solution.py:30
  304.6 5.1 exponential_reduce_fusion.4
  309.7 63.7 %psum.66 = f32[2048]{0:T(1024)S(1)} all-reduce(f32[2048]{0:T(1024)S(1)} %exponential_reduce_fusion.4), channel_id=1, replica_groups=mesh['gen'=32,'beam'=8] {'gen'}, use_global_device_ids=true, to_apply=%region_17.0 | all-reduce | flops 2048 | bytes 16384 | tf_op jit(solution)/shard_map/psum | solution.py:31
  374.0 4.9 fusion.2
  378.9 12.4 %pmax.60 = f32[1024]{0:T(1024)S(1)} all-reduce(f32[1024]{0:T(1024)S(1)} %fusion.2), channel_id=1, replica_groups=mesh['gen'=32,'beam'=8] {'beam'}, use_global_device_ids=true, to_apply=%region_19.0 | all-reduce | flops 1024 | bytes 8192 | tf_op jit(solution)/shard_map/pmax | solution.py:24
  391.3 5.1 exponential_reduce_fusion.3
  396.4 11.1 psum.67
  412.9 70.7 %pmax.61 = f32[2048]{0:T(1024)S(1)} all-reduce(f32[2048]{0:T(1024)S(1)} %fusion.17), channel_id=1, replica_groups=mesh['gen'=32,'beam'=8] {'gen'}, use_global_device_ids=true, to_apply=%region_23.0 | all-reduce | flops 2048 | bytes 16384 | tf_op jit(solution)/shard_map/pmax | solution.py:30
  483.6 5.2 exponential_reduce_fusion.2
  488.7 63.7 %psum.68 = f32[2048]{0:T(1024)S(1)} all-reduce(f32[2048]{0:T(1024)S(1)} %exponential_reduce_fusion.2), channel_id=1, replica_groups=mesh['gen'=32,'beam'=8] {'gen'}, use_global_device_ids=true, to_apply=%region_25.0 | all-reduce | flops 2048 | bytes 16384 | tf_op jit(solution)/shard_map/psum | solution.py:31
  553.1 4.9 fusion.3
  558.0 12.4 %pmax.62 = f32[1024]{0:T(1024)S(1)} all-reduce(f32[1024]{0:T(1024)S(1)} %fusion.3), channel_id=1, replica_groups=mesh['gen'=32,'beam'=8] {'beam'}, use_global_device_ids=true, to_apply=%region_27.0 | all-reduce | flops 1024 | bytes 8192 | tf_op jit(solution)/shard_map/pmax | solution.py:24
  570.4 5.1 exponential_reduce_fusion.1
  575.5 10.9 psum.69
  591.8 70.7 %pmax.63 = f32[2048]{0:T(1024)S(1)} all-reduce(f32[2048]{0:T(1024)S(1)} %fusion.18), channel_id=1, replica_groups=mesh['gen'=32,'beam'=8] {'gen'}, use_global_device_ids=true, to_apply=%region_31.0 | all-reduce | flops 2048 | bytes 16384 | tf_op jit(solution)/shard_map/pmax | solution.py:30
  662.5 5.2 exponential_reduce_fusion
  667.7 63.7 %psum.70 = f32[2048]{0:T(1024)S(1)} all-reduce(f32[2048]{0:T(1024)S(1)} %exponential_reduce_fusion), channel_id=1, replica_groups=mesh['gen'=32,'beam'=8] {'gen'}, use_global_device_ids=true, to_apply=%region_33.0 | all-reduce | flops 2048 | bytes 16384 | tf_op jit(solution)/shard_map/psum | solution.py:31
  732.0 5.7 fusion.37
  746.7 73.1 %reduce-scatter.5.cloned.1.call-done = f32[64,128]{1,0:T(8,128)} async-done(((f32[2048,128]{1,0:T(8,128)}), f32[64,128]{1,0:T(8,128)}) %reduce-scatter.5.cloned.1.call-update) | async-done | bytes 32784 | tf_op jit(solution)/shard_map/reduce_scatter | solution.py:86
  820.9 35.3 %reduce-scatter.3.cloned.1.call-done = f32[128,128]{0,1:T(8,128)} async-done(((f32[1024,128]{0,1:T(8,128)}), f32[128,128]{0,1:T(8,128)}) %reduce-scatter.3.cloned.1.call-update) | async-done | bytes 65552 | tf_op jit(solution)/shard_map/reduce_scatter | solution.py:73
  858.0 248.3 %all-reduce.2.cloned.1.call-done = f32[256,128]{1,0:T(8,128)} async-done(((f32[256,128]{1,0:T(8,128)}), f32[256,128]{1,0:T(8,128)}) %all-reduce.2.cloned.1.call-update) | async-done | bytes 131088 | tf_op jit(solution)/shard_map/psum | solution.py:96
  (34 shorter events, 41.2 us)
Async XLA Ops:
  7.2 1.5 copy-start
  7.2 812.7 %reduce-scatter.5.cloned.1.call-start = ((), (), s32[]{:S(2)}) async-start(), calls=%async_computation.3 | async-start | bytes 1081344 | tf_op jit(solution)/shard_map/reduce_scatter | solution.py:86
  587.1 144.9 %copy-start.2 = (f32[1024]{0:T(1024)}, f32[1024]{0:T(1024)S(1)}, u32[]{:S(2)}) copy-start(f32[1024]{0:T(1024)S(1)} %subtract_multiply_fusion.4) | copy-start | bytes 12292
  732.0 10.0 copy-start.3
  737.7 1.9 copy-start.1
  742.1 114.1 %reduce-scatter.3.cloned.1.call-start = ((), (), s32[]{:S(2)}) async-start(), calls=%async_computation.2 | async-start | bytes 589824 | tf_op jit(solution)/shard_map/reduce_scatter | solution.py:73
  746.7 359.6 %all-reduce.2.cloned.1.call-start = ((), (), s32[]{:S(2)}) async-start(), calls=%async_computation.4 | async-start | bytes 262144 | tf_op jit(solution)/shard_map/psum | solution.py:96
Sparse Core Ops, SparseCore 0:
  742.2 77.6 reduce-scatter.4
  822.5 33.5 reduce-scatter.2
  862.2 243.9 all-reduce.1
where the time goes:
time: 1120 us; the launch traced here: 1110 us
  blocking collectives  636 us (57%)
  waiting for transfers between devices  357 us (32%)
  other arithmetic  85 us (8%)
  matrix products  17.8 us (2%)
  between operations  14 us (1%)
    pmax x4, blocking collectives, col_lse(): top = lax.pmax(jnp.max(scores, axis=0), 'gen')  283 us
    psum x4, blocking collectives, col_lse(): total = lax.psum(jnp.sum(jnp.exp(scores - top[None, :]), axis=0), 'gen')  254 us
    psum x1, waiting for transfers between devices, on_device(): weight_grad = lax.psum(partial_grad, ('gen', 'beam'))  248 us
    reduce_scatter x1, waiting for transfers between devices, on_device(): lax.psum_scatter(2.0 * (col_mass[:, None] * own - moved), 'gen', scatter_...  73.1 us
    pmax x4, blocking collectives, row_lse(): top = lax.pmax(jnp.max(scores, axis=1), 'beam')  54.5 us
    psum x4, blocking collectives, row_lse(): total = lax.psum(jnp.sum(jnp.exp(scores - top[:, None]), axis=1), 'beam')  43.5 us
    reduce_scatter x1, waiting for transfers between devices, on_device(): lax.psum_scatter(2.0 * (row_mass[:, None] * own - moved), 'beam', scatter...  35.3 us
  transfers between devices with their start and end apart: 3, of which 3 were waited for; matrix products, arithmetic and copies ran while one was open for 0% of the time, Pallas kernels for 0%

commit v1 on v0

v1 whole, which is shorter than its diff:
```python
import functools
import math

import jax
import jax.numpy as jnp
from jax import lax
from jax.experimental import pallas as pl
from jax.experimental.pallas import tpu as pltpu
from jax.sharding import PartitionSpec as P

SWEEPS = 4
LOG2E = 1.4426950408889634
BYTES = 24 * 1024 * 1024
NT = (((1,), (1,)), ((), ()))
WIDE = 512
F32 = jnp.float32
BF16 = jnp.bfloat16


def merged(parts, scale):
    count = parts.shape[0]
    top = parts[0]
    for d in range(1, count):
        top = jnp.maximum(top, parts[d])
    total = jnp.exp2((parts[0] - top) * scale)
    for d in range(1, count):
        total = total + jnp.exp2((parts[d] - top) * scale)
    return top + jnp.log2(total) / scale


def as_column(dense):
    turned = jnp.transpose(dense)
    return jnp.concatenate([turned[:, r : r + 1] for r in range(dense.shape[0])], axis=0)


def partial_lse(summed, kept, column, scale, top_scr, sum_scr, out_ref):
    wide = min(WIDE, kept.shape[0])
    tiles = wide // 128

    def step(n, carry):
        right = kept[pl.ds(pl.multiple_of(n * wide, wide), wide), :]
        t = lax.dot_general(summed[...], right, NT, preferred_element_type=F32) + column
        top = jnp.max(t, axis=0, keepdims=True)
        total = jnp.sum(jnp.exp2((t - top) * scale), axis=0, keepdims=True)
        for i in range(tiles):
            top_scr[pl.ds(n * tiles + i, 1), :] = top[:, i * 128 : (i + 1) * 128]
            sum_scr[pl.ds(n * tiles + i, 1), :] = total[:, i * 128 : (i + 1) * 128]
        return carry

    lax.fori_loop(0, kept.shape[0] // wide, step, 0, unroll=2)
    part = top_scr[...] + jnp.log2(sum_scr[...]) / scale
    out_ref[...] = jnp.broadcast_to(part[None], out_ref.shape)


def first_kernel(eps, gen_showers, beam_showers, weight, out, gen_emb, beam_emb, top_scr, sum_scr):
    scale = 2.0 * LOG2E / eps[0]
    gen_emb[...] = jnp.tanh(jnp.dot(gen_showers[...], weight[...], preferred_element_type=F32)).astype(BF16)
    beam = jnp.tanh(jnp.dot(beam_showers[...], weight[...], preferred_element_type=F32)).astype(BF16)
    beam_emb[...] = beam
    beam = beam.astype(F32)
    column = -0.5 * jnp.sum(beam * beam, axis=1, keepdims=True)
    partial_lse(beam_emb, gen_emb, column, scale, top_scr, sum_scr, out)


def pass_kernel(before, now, log_count, eps, parts, summed, kept, out, half, top_scr, sum_scr):
    scale = 2.0 * LOG2E / eps[now]
    found = merged(parts, 2.0 * LOG2E / eps[before])
    dense = eps[before] * (0.5 * log_count) - found
    half[...] = dense
    partial_lse(summed, kept, as_column(dense), scale, top_scr, sum_scr, out)


def turned_kernel(showers, weight, emb_t, slope_t, square):
    act = jnp.tanh(lax.dot_general(weight[...], showers[...], (((0,), (1,)), ((), ())), preferred_element_type=F32))
    emb = act.astype(BF16)
    emb_t[...] = emb
    slope_t[...] = 2.0 * (1.0 - act * act)
    emb = emb.astype(F32)
    line = jnp.sum(emb * emb, axis=0, keepdims=True)
    for r in range(square.shape[0]):
        square[r : r + 1, :] = line[:, r * 128 : (r + 1) * 128]


def exact_dot(left, right):
    one = left.astype(BF16)
    rest = left - one.astype(F32)
    two = rest.astype(BF16)
    three = (rest - two.astype(F32)).astype(BF16)
    out = jnp.dot(jnp.concatenate([one, two, three], axis=0), right, preferred_element_type=F32)
    n = left.shape[0]
    return out[:n] + (out[n : 2 * n] + out[2 * n :])


def last_kernel(
    log_gen, log_beam, eps, parts, gen_half, gen_emb, beam_emb, gen_t, beam_t, gen_slope, beam_slope,
    gen_square, beam_square, gen_showers, beam_showers, gen_pot, beam_pot, grad, moved_gen, rows_scr, line_scr,
):
    e = eps[SWEEPS - 1]
    scale = 2.0 * LOG2E / e
    beam_half = e * (0.5 * log_gen) - merged(parts, scale)
    gen_pot[...] = 2.0 * gen_half[...] + gen_square[...]
    beam_pot[...] = 2.0 * beam_half + beam_square[...]
    shift = beam_half * scale - log_beam * LOG2E
    for r in range(shift.shape[0]):
        line_scr[:, r * 128 : (r + 1) * 128] = shift[r : r + 1, :]
    column = as_column(gen_half[...]) * scale
    moved_gen[...] = jnp.zeros_like(moved_gen)
    rows_scr[...] = jnp.zeros_like(rows_scr)
    wide = 256

    def step(n, carry):
        at = pl.ds(pl.multiple_of(n * wide, wide), wide)
        cross = lax.dot_general(gen_emb[...], beam_emb[at, :], NT, preferred_element_type=F32)
        mass = jnp.exp2(cross * scale + column + line_scr[:, at])
        plan = mass.astype(BF16)
        rows_scr[...] += mass[:, :128] + mass[:, 128:]
        col_mass = jnp.sum(mass, axis=0, keepdims=True)
        moved = jnp.dot(gen_t[...], plan, preferred_element_type=F32)
        pre = (col_mass * beam_t[:, at].astype(F32) - moved) * beam_slope[:, at]
        moved_gen[...] += lax.dot_general(beam_t[:, at], plan, NT, preferred_element_type=F32)
        return carry + exact_dot(pre, beam_showers[at, :])

    total = lax.fori_loop(0, beam_emb.shape[0] // wide, step, jnp.zeros((128, 256), F32))
    row_mass = lax.dot_general(
        jnp.ones((8, 128), F32), rows_scr[...], NT, precision=lax.Precision.HIGHEST, preferred_element_type=F32
    )[:1]
    pre = (row_mass * gen_t[...].astype(F32) - moved_gen[...]) * gen_slope[...]
    total = total + exact_dot(pre, gen_showers[...])
    grad[...] = jnp.transpose(total)


SCALARS = pl.BlockSpec(memory_space=pltpu.SMEM)
LOCAL = pl.BlockSpec(memory_space=pltpu.VMEM)


def call(kernel, operands, outs, scratch=()):
    return pl.pallas_call(
        kernel,
        out_shape=tuple(jax.ShapeDtypeStruct(*o) for o in outs),
        in_specs=[SCALARS if a.ndim == 1 else LOCAL for a in operands],
        out_specs=tuple(LOCAL for _ in outs),
        scratch_shapes=[pltpu.VMEM(*s) for s in scratch],
        compiler_params=pltpu.CompilerParams(vmem_limit_bytes=BYTES),
    )(*operands)


def swap(x, axis):
    return lax.all_to_all(x, axis, split_axis=0, concat_axis=0, tiled=True)


def on_device(gen_showers, beam_showers, embed_weight, eps_roster):
    gens, beams = lax.axis_size("gen"), lax.axis_size("beam")
    rows, columns = gen_showers.shape[0], beam_showers.shape[0]
    depth, width = embed_weight.shape
    log_gen, log_beam = math.log(rows * gens), math.log(columns * beams)
    r, c = rows // 128, columns // 128
    gen_scratch = [((r, 128), F32)] * 2
    beam_scratch = [((c, 128), F32)] * 2
    gen_parts, gen_emb, beam_emb = call(
        first_kernel,
        (eps_roster, gen_showers, beam_showers, embed_weight),
        [((beams, r, 128), F32), ((rows, width), BF16), ((columns, width), BF16)],
        gen_scratch,
    )
    gen_t, gen_slope, gen_square = call(
        turned_kernel,
        (gen_showers, embed_weight),
        [((width, rows), BF16), ((width, rows), F32), ((r, 128), F32)],
    )
    beam_t, beam_slope, beam_square = call(
        turned_kernel,
        (beam_showers, embed_weight),
        [((width, columns), BF16), ((width, columns), F32), ((c, 128), F32)],
    )
    for sweep in range(SWEEPS):
        if sweep:
            gen_parts, unused = call(
                functools.partial(pass_kernel, sweep - 1, sweep, log_gen),
                (eps_roster, beam_parts, beam_emb, gen_emb),
                [((beams, r, 128), F32), ((c, 128), F32)],
                gen_scratch,
            )
        gen_parts = swap(gen_parts, "beam")
        beam_parts, gen_half = call(
            functools.partial(pass_kernel, sweep, sweep, log_beam),
            (eps_roster, gen_parts, gen_emb, beam_emb),
            [((gens, c, 128), F32), ((r, 128), F32)],
            beam_scratch,
        )
        beam_parts = swap(beam_parts, "gen")
    gen_pot, beam_pot, grad = call(
        functools.partial(last_kernel, log_gen, log_beam),
        (
            eps_roster, beam_parts, gen_half, gen_emb, beam_emb, gen_t, beam_t, gen_slope, beam_slope,
            gen_square, beam_square, gen_showers, beam_showers,
        ),
        [((r, 128), F32), ((c, 128), F32), ((depth, width), F32)],
        [((width, rows), F32), ((rows, 128), F32), ((1, columns), F32)],
    )
    piece = swap(grad.reshape(gens, depth // gens, width), "gen").sum(0)
    piece = swap(jnp.broadcast_to(piece[None], (beams,) + piece.shape), "beam").sum(0)
    grad = swap(jnp.broadcast_to(piece[None], (gens,) + piece.shape), "gen")
    return gen_pot.reshape(rows), beam_pot.reshape(columns), grad.reshape(depth, width)


def solution(mesh):
    in_specs = (P("gen", None), P("beam", None), P(), P())
    out_specs = (P("gen"), P("beam"), P())
    return jax.shard_map(on_device, mesh=mesh, in_specs=in_specs, out_specs=out_specs, check_vma=False)
```

time: 1120 us -> 187 us (0.17)
  blocking collectives: 636 us -> 121 us
  waiting for transfers between devices: 357 us -> 5.76 us
  other arithmetic: 85 us -> 0.05 us
  Pallas kernels: 0 us -> 41.7 us
  matrix products: 17.8 us -> 0 us
  between operations: 14 us -> 0.72 us
    pmax x8 -> x0, blocking collectives: 338 us -> none  [the longest x4 283 us: col_lse(): top = lax.pmax(jnp.max(scores, axis=0), 'gen')]
    psum x8 -> x0, blocking collectives: 298 us -> none  [the longest x4 254 us: col_lse(): total = lax.psum(jnp.sum(jnp.exp(scores - top[None, :]), axis=0), 'gen')]
    psum x1 -> x0, waiting for transfers between devices: 248 us -> none  [on_device(): weight_grad = lax.psum(partial_grad, ('gen', 'beam'))]
    all_to_all x0 -> x10, blocking collectives: none -> 121 us  [swap(): return lax.all_to_all(x, axis, split_axis=0, concat_axis=0, tiled=True)]
    reduce_scatter x2 -> x0, waiting for transfers between devices: 108 us -> none  [the longest x1 73.1 us: on_device(): lax.psum_scatter(2.0 * (col_mass[:, None] * own - moved), 'gen', scatter_...]
    reduce_sum x9 -> x2, other arithmetic: 46.7 us -> 0.05 us  [the longest x1 0.04 us: on_device(): piece = swap(grad.reshape(gens, depth // gens, width), 'gen').sum(0)]
    pallas_call x0 -> x11, Pallas kernels: none -> 41.7 us  [call(): pl.pallas_call(kernel, out_shape=tuple((jax.ShapeDtypeStruct(*o) for o in...]
    reduce_max x7 -> x0, other arithmetic: 33.3 us -> none  [the longest x4 18.6 us: col_lse(): top = lax.pmax(jnp.max(scores, axis=0), 'gen')]
  transfers between devices with their start and end apart: 3 -> 1, of which waited for: 3 -> 1; matrix products, arithmetic and copies ran while one was open for 0% -> 0% of each run, Pallas kernels for 0% -> 1%
where the time goes in v1:
time: 187 us; the launch traced here: 186 us
  blocking collectives  121 us (65%)
  Pallas kernels  41.7 us (22%)
  local copies, waits for them, and re-layouts  10.4 us (6%)
  waiting for transfers between devices  5.76 us (3%)
  starting transfers between devices  5.69 us (3%)
    all_to_all x10, blocking collectives, swap(): return lax.all_to_all(x, axis, split_axis=0, concat_axis=0, tiled=True)  121 us
    pallas_call x11, Pallas kernels, call(): pl.pallas_call(kernel, out_shape=tuple((jax.ShapeDtypeStruct(*o) for o in...  41.7 us
    unnamed x29, local copies, waits for them, and re-layouts  10.4 us
    all_to_all x1, waiting for transfers between devices, swap(): return lax.all_to_all(x, axis, split_axis=0, concat_axis=0, tiled=True)  5.76 us
    all_to_all x1, starting transfers between devices, swap(): return lax.all_to_all(x, axis, split_axis=0, concat_axis=0, tiled=True)  5.69 us
  transfers between devices with their start and end apart: 1, of which 1 were waited for; matrix products, arithmetic and copies ran while one was open for 0% of the time, Pallas kernels for 1%

profile of v1, /device:TPU:1, one launch (start us, length us, event | category | flops | bytes accessed | tf_op | source)
XLA Modules:
  0.0 185.7 jit_solution(6725412294535329237)
XLA Ops:
  0.6 1.2 copy-done
  1.9 1.0 copy-done.2
  2.9 0.8 copy-done.4
  4.4 4.3 %shard_map.67 = (f32[8,8,128]{2,1,0:T(8,128)S(1)}, bf16[1024,128]{1,0:T(8,128)(2,1)S(1)}, bf16[2048,128]{1,0:T(8,128)(2,1)S(1)}) custom-call(f32[4]{0:T(128)S(1)} %copy-done.12, bf16[1024,256]{1,0:T(8,128)(2,1)S(1)} %copy-done.2, bf16[2048,256]{1,0:T(8,128)(2,1)S(1)} %copy-done, bf16[256,128]{1,0:T(8,128)(2,1)S(1)} %copy-done.4), custom_call_target="tpu_custom_call" | custom-call | tf_op jit(solution)/shard_map/pallas_call | solution.py:137
  8.7 15.7 %all_to_all.55.parts = f32[8,8,128]{2,1,0:T(8,128)S(1)} all-to-all(f32[8,8,128]{2,1,0:T(8,128)S(1)} %get-tuple-element.23), channel_id=1, replica_groups=mesh['gen'=32,'beam'=8] {'beam'}, dimensions={0} | all-to-all | bytes 65536 | tf_op jit(solution)/shard_map/all_to_all | solution.py:148
  24.3 4.1 %shard_map.68 = (f32[32,16,128]{2,1,0:T(8,128)S(1)}, f32[8,128]{1,0:T(8,128)}) custom-call(f32[4]{0:T(128)S(1)} %copy-done.12, f32[8,8,128]{2,1,0:T(8,128)S(1)} %all_to_all.55.parts, bf16[1024,128]{1,0:T(8,128)(2,1)S(1)} %get-tuple-element.24.summed.kept.gen_emb, bf16[2048,128]{1,0:T(8,128)(2,1)S(1)} %get-tuple-element.25.kept.summed.beam_emb), custom_call_target="tpu_custom_call" | custom-call | tf_op jit(solution)/shard_map/pallas_call | solution.py:137
  28.5 17.9 %all_to_all.56.parts = f32[32,16,128]{2,1,0:T(8,128)S(1)} all-to-all(f32[32,16,128]{2,1,0:T(8,128)S(1)} %get-tuple-element.26), channel_id=1, replica_groups=mesh['gen'=32,'beam'=8] {'gen'}, dimensions={0} | all-to-all | bytes 524288 | tf_op jit(solution)/shard_map/all_to_all | solution.py:148
  46.4 3.5 %shard_map.69 = (f32[8,8,128]{2,1,0:T(8,128)S(1)}, f32[16,128]{1,0:T(8,128)}) custom-call(f32[4]{0:T(128)S(1)} %copy-done.12, f32[32,16,128]{2,1,0:T(8,128)S(1)} %all_to_all.56.parts, bf16[2048,128]{1,0:T(8,128)(2,1)S(1)} %get-tuple-element.25.kept.summed.beam_emb, bf16[1024,128]{1,0:T(8,128)(2,1)S(1)} %get-tuple-element.24.summed.kept.gen_emb), custom_call_target="tpu_custom_call" | custom-call | tf_op jit(solution)/shard_map/pallas_call | solution.py:137
  49.9 9.2 %all_to_all.57.parts = f32[8,8,128]{2,1,0:T(8,128)S(1)} all-to-all(f32[8,8,128]{2,1,0:T(8,128)S(1)} %get-tuple-element.27), channel_id=1, replica_groups=mesh['gen'=32,'beam'=8] {'beam'}, dimensions={0} | all-to-all | bytes 65536 | tf_op jit(solution)/shard_map/all_to_all | solution.py:148
  59.1 4.1 %shard_map.70 = (f32[32,16,128]{2,1,0:T(8,128)S(1)}, f32[8,128]{1,0:T(8,128)}) custom-call(f32[4]{0:T(128)S(1)} %copy-done.12, f32[8,8,128]{2,1,0:T(8,128)S(1)} %all_to_all.57.parts, bf16[1024,128]{1,0:T(8,128)(2,1)S(1)} %get-tuple-element.24.summed.kept.gen_emb, bf16[2048,128]{1,0:T(8,128)(2,1)S(1)} %get-tuple-element.25.kept.summed.beam_emb), custom_call_target="tpu_custom_call" | custom-call | tf_op jit(solution)/shard_map/pallas_call | solution.py:137
  63.2 13.6 %all_to_all.58.parts = f32[32,16,128]{2,1,0:T(8,128)S(1)} all-to-all(f32[32,16,128]{2,1,0:T(8,128)S(1)} %get-tuple-element.28), channel_id=1, replica_groups=mesh['gen'=32,'beam'=8] {'gen'}, dimensions={0} | all-to-all | bytes 524288 | tf_op jit(solution)/shard_map/all_to_all | solution.py:148
  76.8 3.5 %shard_map.71 = (f32[8,8,128]{2,1,0:T(8,128)S(1)}, f32[16,128]{1,0:T(8,128)}) custom-call(f32[4]{0:T(128)S(1)} %copy-done.12, f32[32,16,128]{2,1,0:T(8,128)S(1)} %all_to_all.58.parts, bf16[2048,128]{1,0:T(8,128)(2,1)S(1)} %get-tuple-element.25.kept.summed.beam_emb, bf16[1024,128]{1,0:T(8,128)(2,1)S(1)} %get-tuple-element.24.summed.kept.gen_emb), custom_call_target="tpu_custom_call" | custom-call | tf_op jit(solution)/shard_map/pallas_call | solution.py:137
  80.3 9.2 %all_to_all.59.parts = f32[8,8,128]{2,1,0:T(8,128)S(1)} all-to-all(f32[8,8,128]{2,1,0:T(8,128)S(1)} %get-tuple-element.29), channel_id=1, replica_groups=mesh['gen'=32,'beam'=8] {'beam'}, dimensions={0} | all-to-all | bytes 65536 | tf_op jit(solution)/shard_map/all_to_all | solution.py:148
  89.6 4.1 %shard_map.72 = (f32[32,16,128]{2,1,0:T(8,128)S(1)}, f32[8,128]{1,0:T(8,128)}) custom-call(f32[4]{0:T(128)S(1)} %copy-done.12, f32[8,8,128]{2,1,0:T(8,128)S(1)} %all_to_all.59.parts, bf16[1024,128]{1,0:T(8,128)(2,1)S(1)} %get-tuple-element.24.summed.kept.gen_emb, bf16[2048,128]{1,0:T(8,128)(2,1)S(1)} %get-tuple-element.25.kept.summed.beam_emb), custom_call_target="tpu_custom_call" | custom-call | tf_op jit(solution)/shard_map/pallas_call | solution.py:137
  93.7 13.6 %all_to_all.60.parts = f32[32,16,128]{2,1,0:T(8,128)S(1)} all-to-all(f32[32,16,128]{2,1,0:T(8,128)S(1)} %get-tuple-element.30), channel_id=1, replica_groups=mesh['gen'=32,'beam'=8] {'gen'}, dimensions={0} | all-to-all | bytes 524288 | tf_op jit(solution)/shard_map/all_to_all | solution.py:148
  107.3 3.5 %shard_map.73 = (f32[8,8,128]{2,1,0:T(8,128)S(1)}, f32[16,128]{1,0:T(8,128)}) custom-call(f32[4]{0:T(128)S(1)} %copy-done.12, f32[32,16,128]{2,1,0:T(8,128)S(1)} %all_to_all.60.parts, bf16[2048,128]{1,0:T(8,128)(2,1)S(1)} %get-tuple-element.25.kept.summed.beam_emb, bf16[1024,128]{1,0:T(8,128)(2,1)S(1)} %get-tuple-element.24.summed.kept.gen_emb), custom_call_target="tpu_custom_call" | custom-call | tf_op jit(solution)/shard_map/pallas_call | solution.py:137
  110.8 9.4 %all_to_all.61.parts = f32[8,8,128]{2,1,0:T(8,128)S(1)} all-to-all(f32[8,8,128]{2,1,0:T(8,128)S(1)} %get-tuple-element.31), channel_id=1, replica_groups=mesh['gen'=32,'beam'=8] {'beam'}, dimensions={0} | all-to-all | bytes 65536 | tf_op jit(solution)/shard_map/all_to_all | solution.py:148
  120.2 4.5 %shard_map.74 = (f32[32,16,128]{2,1,0:T(8,128)}, f32[8,128]{1,0:T(8,128)S(1)}) custom-call(f32[4]{0:T(128)S(1)} %copy-done.12, f32[8,8,128]{2,1,0:T(8,128)S(1)} %all_to_all.61.parts, bf16[1024,128]{1,0:T(8,128)(2,1)S(1)} %get-tuple-element.24.summed.kept.gen_emb, bf16[2048,128]{1,0:T(8,128)(2,1)S(1)} %get-tuple-element.25.kept.summed.beam_emb), custom_call_target="tpu_custom_call" | custom-call | tf_op jit(solution)/shard_map/pallas_call | solution.py:137
  124.7 5.7 %all-to-all-start.7 = ((f32[32,16,128]{2,1,0:T(8,128)}), f32[32,16,128]{2,1,0:T(8,128)}, u32[]{:S(2)}, u32[]{:S(2)}) async-start(f32[32,16,128]{2,1,0:T(8,128)} %get-tuple-element.32), calls=%async_computation.7 | async-start | bytes 524288 | tf_op jit(solution)/shard_map/all_to_all | solution.py:148
  130.8 0.8 copy-done.6
  131.6 0.7 copy-done.10
  132.9 0.8 copy-done.8
  133.7 5.8 %all-to-all-done.7.parts = f32[32,16,128]{2,1,0:T(8,128)} async-done(((f32[32,16,128]{2,1,0:T(8,128)}), f32[32,16,128]{2,1,0:T(8,128)}, u32[]{:S(2)}, u32[]{:S(2)}) %all-to-all-start.7) | async-done | bytes 262176 | tf_op jit(solution)/shard_map/all_to_all | solution.py:148
  139.4 0.7 copy-done.13
  140.1 1.0 copy-done.7
  141.1 1.0 copy-done.9
  142.2 0.9 copy-done.11
  143.1 9.0 %shard_map.77 = (f32[8,128]{1,0:T(8,128)}, f32[16,128]{1,0:T(8,128)}, f32[256,128]{1,0:T(8,128)S(1)}) custom-call(f32[4]{0:T(128)S(1)} %copy-done.13, f32[32,16,128]{2,1,0:T(8,128)} %all-to-all-done.7.parts, f32[8,128]{1,0:T(8,128)S(1)} %get-tuple-element.33.gen_half, bf16[1024,128]{1,0:T(8,128)(2,1)S(1)} %get-tuple-element.24.summed.kept.gen_emb, ...), custom_call_target="tpu_custom_call" | custom-call | tf_op jit(solution)/shard_map/pallas_call | solution.py:137
  152.2 11.2 %all_to_all.62 = f32[32,8,128]{2,1,0:T(8,128)S(1)} all-to-all(f32[32,8,128]{2,1,0:T(8,128)S(1)} %bitcast.4), channel_id=1, replica_groups=mesh['gen'=32,'beam'=8] {'gen'}, dimensions={0} | all-to-all | bytes 262144 | tf_op jit(solution)/shard_map/all_to_all | solution.py:148
  163.4 9.2 %all_to_all.63 = f32[8,8,128]{2,1,0:T(8,128)S(1)} all-to-all(f32[8,8,128]{2,1,0:T(8,128)S(1)} %broadcast_in_dim.4), channel_id=1, replica_groups=mesh['gen'=32,'beam'=8] {'beam'}, dimensions={0} | all-to-all | bytes 65536 | tf_op jit(solution)/shard_map/all_to_all | solution.py:148
  172.6 12.4 %all_to_all.64 = f32[32,8,128]{2,1,0:T(8,128)S(1)} all-to-all(f32[32,8,128]{2,1,0:T(8,128)S(1)} %broadcast_in_dim.5), channel_id=1, replica_groups=mesh['gen'=32,'beam'=8] {'gen'}, dimensions={0} | all-to-all | bytes 262144 | tf_op jit(solution)/shard_map/all_to_all | solution.py:148
  185.1 0.7 copy.8
  (24 shorter events, 1.7 us)
Async XLA Ops:
  0.6 1.2 copy-start
  1.9 1.0 copy-start.2
  2.9 0.8 copy-start.4
  3.7 0.7 copy-start.12
  107.3 23.1 %copy-start.3 = (bf16[1024,256]{1,0:T(8,128)(2,1)S(1)}, bf16[1024,256]{1,0:T(8,128)(2,1)}, u32[]{:S(2)}) copy-start(bf16[1024,256]{1,0:T(8,128)(2,1)} %gen_showers.3) | copy-start | bytes 1572868
  110.8 21.5 %copy-start.1 = (bf16[2048,256]{1,0:T(8,128)(2,1)S(1)}, bf16[2048,256]{1,0:T(8,128)(2,1)}, u32[]{:S(2)}) copy-start(bf16[2048,256]{1,0:T(8,128)(2,1)} %beam_showers.3) | copy-start | bytes 3145732
  124.7 5.7 %copy-start.5 = (bf16[256,128]{1,0:T(8,128)(2,1)S(1)}, bf16[256,128]{1,0:T(8,128)(2,1)}, u32[]{:S(2)}) copy-start(bf16[256,128]{1,0:T(8,128)(2,1)} %weight.5) | copy-start | bytes 196612
  124.7 14.7 %all-to-all-start.7 = ((f32[32,16,128]{2,1,0:T(8,128)}), f32[32,16,128]{2,1,0:T(8,128)}, u32[]{:S(2)}, u32[]{:S(2)}) async-start(f32[32,16,128]{2,1,0:T(8,128)} %get-tuple-element.32), calls=%async_computation.7 | async-start | bytes 524288 | tf_op jit(solution)/shard_map/all_to_all | solution.py:148
  130.8 0.8 copy-start.6
  131.6 0.7 copy-start.10
  132.9 0.8 copy-start.8
  139.4 0.7 copy-start.13
  140.1 1.0 copy-start.7
  141.1 1.0 copy-start.9
  142.2 0.9 copy-start.11

commit v2 on v1

v2 whole, which is shorter than its diff:
```python
import functools
import math

import jax
import jax.numpy as jnp
from jax import lax
from jax.experimental import pallas as pl
from jax.experimental.pallas import tpu as pltpu
from jax.sharding import PartitionSpec as P

SWEEPS = 4
LOG2E = 1.4426950408889634
BYTES = 16 * 1024 * 1024
FIRST_BYTES = 20 * 1024 * 1024
NT = (((1,), (1,)), ((), ()))
F32 = jnp.float32
BF16 = jnp.bfloat16
WIDE = 256
BLOCK = 64
DEEP = 512


def merged(parts, scale):
    count = parts.shape[0]
    top = parts[0]
    for d in range(1, count):
        top = jnp.maximum(top, parts[d])
    total = jnp.exp2((parts[0] - top) * scale)
    for d in range(1, count):
        total = total + jnp.exp2((parts[d] - top) * scale)
    return top + jnp.log2(total) / scale


def spread(dense, column):
    turned = jnp.transpose(dense)
    for r in range(dense.shape[0]):
        column[r * 128 : (r + 1) * 128, :] = jnp.broadcast_to(turned[:, r : r + 1], (128, 128))


def partial_lse(cross, column, scale, top_scr, sum_scr, out, factors=None, kernel=None):
    rows, lanes = cross.shape
    count, tiles = lanes // WIDE, WIDE // 128

    def lift(r):
        return jnp.concatenate([column[r : r + BLOCK, :]] * tiles, axis=1)

    def fold(x, op):
        return op(x.reshape(BLOCK // 8, 8, WIDE), axis=0)

    def put(scr, n, line):
        for i in range(tiles):
            scr[n * tiles + i : n * tiles + i + 1, :] = line[:, i * 128 : (i + 1) * 128]

    last = None
    for n in range(count + 1):
        new, old = slice(n * WIDE, (n + 1) * WIDE), slice((n - 1) * WIDE, n * WIDE)
        top = total = None
        for r in range(0, rows, BLOCK):
            at = slice(r, r + BLOCK)
            if n < count:
                if factors is None:
                    t = cross[at, new]
                else:
                    if r % DEEP == 0:
                        summed, kept = factors
                        made = lax.dot_general(summed[r : r + DEEP, :], kept[new, :], NT, preferred_element_type=F32)
                    t = made[r % DEEP : r % DEEP + BLOCK]
                    cross[at, new] = t
                t = fold(t + lift(r), jnp.max)
                top = t if top is None else jnp.maximum(top, t)
            if n > 0:
                p = jnp.exp2((cross[at, old] + lift(r) - last) * scale)
                if kernel is not None:
                    kernel[at, old] = p
                p = fold(p, jnp.sum)
                total = p if total is None else total + p
        if n > 0:
            put(sum_scr, n - 1, jnp.sum(total, axis=0, keepdims=True))
        if n < count:
            last = jnp.max(top, axis=0, keepdims=True)
            put(top_scr, n, last)
    part = top_scr[...] + jnp.log2(sum_scr[...]) / scale
    out[...] = jnp.broadcast_to(part[None], out.shape)


def embed(showers, weight, emb, slope):
    act = jnp.tanh(jnp.dot(showers[...], weight[...], preferred_element_type=F32))
    emb[...] = act.astype(BF16)
    slope[...] = 2.0 * (1.0 - act * act)


def first_kernel(
    eps, gen_far, beam_far, weight_far, out, gen_emb, beam_emb, gen_slope, gen_t, beam_t, gen_showers_t, beam_showers_t,
    gen_square, beam_square, beam_slope_t, column, top_scr, sum_scr, cross, beam_slope, gen_showers, beam_showers,
    weight, sems,
):
    copies = [
        pltpu.make_async_copy(src, dst, sems.at[i])
        for i, (src, dst) in enumerate(((weight_far, weight), (beam_far, beam_showers), (gen_far, gen_showers)))
    ]
    for copy in copies:
        copy.start()
    copies[0].wait()
    copies[1].wait()
    embed(beam_showers, weight, beam_emb, beam_slope)
    beam = beam_emb[...].astype(F32)
    column[...] = jnp.broadcast_to(-0.5 * jnp.sum(beam * beam, axis=1, keepdims=True), column.shape)
    copies[2].wait()
    embed(gen_showers, weight, gen_emb, gen_slope)
    partial_lse(cross, column, 2.0 * LOG2E / eps[0], top_scr, sum_scr, out, (beam_emb, gen_emb))
    turn(gen_emb, gen_showers, None, gen_t, gen_showers_t, gen_square)
    turn(beam_emb, beam_showers, beam_slope, beam_t, beam_showers_t, beam_square, beam_slope_t)


def made_kernel(before, now, log_count, eps, parts, summed, kept, out, cross, column, top_scr, sum_scr):
    found = merged(parts, 2.0 * LOG2E / eps[before])
    spread(eps[before] * (0.5 * log_count) - found, column)
    partial_lse(cross, column, 2.0 * LOG2E / eps[now], top_scr, sum_scr, out, (summed, kept))


def pass_kernel(before, now, log_count, eps, parts, cross, out, column, top_scr, sum_scr):
    found = merged(parts, 2.0 * LOG2E / eps[before])
    spread(eps[before] * (0.5 * log_count) - found, column)
    partial_lse(cross, column, 2.0 * LOG2E / eps[now], top_scr, sum_scr, out)


def kept_kernel(before, now, log_count, eps, parts, cross, out, kernel, stats, column):
    found = merged(parts, 2.0 * LOG2E / eps[before])
    spread(eps[before] * (0.5 * log_count) - found, column)
    half = stats.shape[0] // 2
    tops, sums = stats.at[pl.ds(0, half)], stats.at[pl.ds(half, half)]
    partial_lse(cross, column, 2.0 * LOG2E / eps[now], tops, sums, out, None, kernel)


def turn(emb, showers, slope, emb_t, showers_t, square, slope_t=None):
    for r in range(square.shape[0]):
        at = slice(r * 128, (r + 1) * 128)
        turned = jnp.transpose(emb[at, :])
        emb_t[:, at] = turned
        turned = turned.astype(F32)
        square[r : r + 1, :] = jnp.sum(turned * turned, axis=0, keepdims=True)
        showers_t[:, at] = jnp.transpose(showers[at, :])
        if slope_t is not None:
            slope_t[:, at] = jnp.transpose(slope[at, :])


def thirds(x, axis):
    one = x.astype(BF16)
    rest = x - one.astype(F32)
    two = rest.astype(BF16)
    return jnp.concatenate([one, two, (rest - two.astype(F32)).astype(BF16)], axis=axis)


def folded(x):
    n = x.shape[1] // 3
    return x[:, :n] + (x[:, n : 2 * n] + x[:, 2 * n :])


def last_kernel(
    log_gen, log_beam, eps, parts, gen_parts, kernel, stats, gen_emb, beam_emb, gen_t, beam_t, gen_slope, beam_slope,
    gen_square, beam_square, gen_showers_t, beam_showers_t, gen_pot, beam_pot, grad, rows_scr, moved_scr,
):
    e = eps[SWEEPS - 1]
    scale = 2.0 * LOG2E / e
    beam_half = e * (0.5 * log_gen) - merged(parts, scale)
    gen_pot[...] = e * log_beam - 2.0 * merged(gen_parts, scale) + gen_square[...]
    beam_pot[...] = 2.0 * beam_half + beam_square[...]
    count = stats.shape[0] // 2
    factor = jnp.exp2((stats[:count, :] + beam_half) * scale - log_beam * LOG2E)
    col_mass = stats[count:, :] * factor
    tiles = WIDE // 128

    def line(dense, n):
        return jnp.concatenate([dense[n * tiles + i : n * tiles + i + 1, :] for i in range(tiles)], axis=1)

    total = None
    for n in range(kernel.shape[1] // WIDE):
        at = slice(n * WIDE, (n + 1) * WIDE)
        mass = kernel[:, at] * line(factor, n)
        plan = mass.astype(BF16)
        sums = mass[:, :128]
        for i in range(1, tiles):
            sums = sums + mass[:, i * 128 : (i + 1) * 128]
        moved = jnp.dot(plan, beam_emb[at, :], preferred_element_type=F32)
        if n == 0:
            rows_scr[...] = sums
            moved_scr[...] = moved
        else:
            rows_scr[...] += sums
            moved_scr[...] += moved
        moved = jnp.dot(gen_t[...], plan, preferred_element_type=F32)
        pre = (line(col_mass, n) * beam_t[:, at].astype(F32) - moved) * beam_slope[:, at]
        part = lax.dot_general(beam_showers_t[:, at], thirds(pre, 0), NT, preferred_element_type=F32)
        total = part if total is None else total + part
    row_mass = jnp.sum(rows_scr[...], axis=1, keepdims=True)
    pre = (row_mass * gen_emb[...].astype(F32) - moved_scr[...]) * gen_slope[...]
    total = total + jnp.dot(gen_showers_t[...], thirds(pre, 1), preferred_element_type=F32)
    grad[...] = folded(total)


SCALARS = pl.BlockSpec(memory_space=pltpu.SMEM)
LOCAL = pl.BlockSpec(memory_space=pltpu.VMEM)
FAR = pl.BlockSpec(memory_space=pltpu.HBM)


def call(kernel, operands, outs, scratch=(), far=(), sems=0, limit=BYTES):
    specs = [SCALARS if a.ndim == 1 else FAR if i in far else LOCAL for i, a in enumerate(operands)]
    scratch = [pltpu.VMEM(*s) for s in scratch]
    if sems:
        scratch.append(pltpu.SemaphoreType.DMA((sems,)))
    return pl.pallas_call(
        kernel,
        out_shape=tuple(jax.ShapeDtypeStruct(*o) for o in outs),
        in_specs=specs,
        out_specs=tuple(LOCAL for _ in outs),
        scratch_shapes=scratch,
        compiler_params=pltpu.CompilerParams(vmem_limit_bytes=limit),
    )(*operands)


def swap(x, axis):
    return lax.all_to_all(x, axis, split_axis=0, concat_axis=0, tiled=True)


def on_device(gen_showers, beam_showers, embed_weight, eps_roster):
    gens, beams = lax.axis_size("gen"), lax.axis_size("beam")
    rows, columns = gen_showers.shape[0], beam_showers.shape[0]
    depth, width = embed_weight.shape
    log_gen, log_beam = math.log(rows * gens), math.log(columns * beams)
    r, c = rows // 128, columns // 128
    gen_out, beam_out = ((beams, r, 128), F32), ((gens, c, 128), F32)
    gen_scratch = [((columns, 128), F32), ((r, 128), F32), ((r, 128), F32)]
    beam_scratch = [((rows, 128), F32), ((c, 128), F32), ((c, 128), F32)]
    (
        gen_parts, gen_emb, beam_emb, gen_slope, gen_t, beam_t, gen_showers_t, beam_showers_t, gen_square, beam_square,
        beam_slope,
    ) = call(
        first_kernel,
        (eps_roster, gen_showers, beam_showers, embed_weight),
        [
            gen_out, ((rows, width), BF16), ((columns, width), BF16), ((rows, width), F32), ((width, rows), BF16),
            ((width, columns), BF16), ((depth, rows), BF16), ((depth, columns), BF16), ((r, 128), F32),
            ((c, 128), F32), ((width, columns), F32),
        ],
        gen_scratch
        + [((columns, rows), F32), ((columns, width), F32)]
        + [(a.shape, BF16) for a in (gen_showers, beam_showers, embed_weight)],
        far=(1, 2, 3),
        sems=3,
        limit=FIRST_BYTES,
    )
    gen_parts = swap(gen_parts, "beam")
    beam_parts, cross = call(
        functools.partial(made_kernel, 0, 0, log_beam),
        (eps_roster, gen_parts, gen_emb, beam_emb),
        [beam_out, ((rows, columns), F32)],
        beam_scratch,
    )
    for sweep in range(1, SWEEPS):
        beam_parts = swap(beam_parts, "gen")
        if sweep == 1:
            gen_parts, turned_cross = call(
                functools.partial(made_kernel, sweep - 1, sweep, log_gen),
                (eps_roster, beam_parts, beam_emb, gen_emb),
                [gen_out, ((columns, rows), F32)],
                gen_scratch,
            )
        else:
            (gen_parts,) = call(
                functools.partial(pass_kernel, sweep - 1, sweep, log_gen),
                (eps_roster, beam_parts, turned_cross),
                [gen_out],
                gen_scratch,
            )
        gen_parts = swap(gen_parts, "beam")
        if sweep < SWEEPS - 1:
            (beam_parts,) = call(
                functools.partial(pass_kernel, sweep, sweep, log_beam),
                (eps_roster, gen_parts, cross),
                [beam_out],
                beam_scratch,
            )
        else:
            beam_parts, kernel, stats = call(
                functools.partial(kept_kernel, sweep, sweep, log_beam),
                (eps_roster, gen_parts, cross),
                [beam_out, ((rows, columns), F32), ((2 * c, 128), F32)],
                beam_scratch[:1],
            )
    beam_parts = swap(beam_parts, "gen")
    gen_pot, beam_pot, grad = call(
        functools.partial(last_kernel, log_gen, log_beam),
        (
            eps_roster, beam_parts, gen_parts, kernel, stats, gen_emb, beam_emb, gen_t, beam_t, gen_slope, beam_slope,
            gen_square, beam_square, gen_showers_t, beam_showers_t,
        ),
        [((r, 128), F32), ((c, 128), F32), ((depth, width), F32)],
        [((rows, 128), F32), ((rows, width), F32)],
    )
    piece = swap(grad.reshape(gens, depth // gens, width), "gen").sum(0)
    piece = swap(jnp.broadcast_to(piece[None], (beams,) + piece.shape), "beam").sum(0)
    grad = swap(jnp.broadcast_to(piece[None], (gens,) + piece.shape), "gen")
    return gen_pot.reshape(rows), beam_pot.reshape(columns), grad.reshape(depth, width)


def solution(mesh):
    in_specs = (P("gen", None), P("beam", None), P(), P())
    out_specs = (P("gen"), P("beam"), P())
    return jax.shard_map(on_device, mesh=mesh, in_specs=in_specs, out_specs=out_specs, check_vma=False)
```

time: 187 us -> 172 us (0.920)
  blocking collectives: 121 us -> 135 us
  Pallas kernels: 41.7 us -> 31 us
  local copies, waits for them, and re-layouts: 10.4 us -> 4.43 us
  waiting for transfers between devices: 5.76 us -> 0 us
  starting transfers between devices: 5.69 us -> 0 us
    all_to_all x10 -> x11, blocking collectives: 121 us -> 135 us  [swap(): return lax.all_to_all(x, axis, split_axis=0, concat_axis=0, tiled=True)]
    pallas_call x11 -> x9, Pallas kernels: 41.7 us -> 31 us  [call(): pl.pallas_call(kernel, out_shape=tuple((jax.ShapeDtypeStruct(*o) for o in...]
    unnamed x29 -> x9, local copies, waits for them, and re-layouts: 10.4 us -> 4.41 us
    all_to_all x1 -> x0, waiting for transfers between devices: 5.76 us -> none  [swap(): return lax.all_to_all(x, axis, split_axis=0, concat_axis=0, tiled=True)]
    all_to_all x1 -> x0, starting transfers between devices: 5.69 us -> none  [swap(): return lax.all_to_all(x, axis, split_axis=0, concat_axis=0, tiled=True)]
  transfers between devices with their start and end apart: 1 -> 0, of which waited for: 1 -> 0; matrix products, arithmetic and copies ran while one was open for 0% -> 0% of each run, Pallas kernels for 1% -> 0%
where the time goes in v2:
time: 172 us; the launch traced here: 171 us
  blocking collectives  135 us (78%)
  Pallas kernels  31 us (18%)
  local copies, waits for them, and re-layouts  4.43 us (3%)
    all_to_all x11, blocking collectives, swap(): return lax.all_to_all(x, axis, split_axis=0, concat_axis=0, tiled=True)  135 us
    pallas_call x9, Pallas kernels, call(): pl.pallas_call(kernel, out_shape=tuple((jax.ShapeDtypeStruct(*o) for o in...  31 us
    unnamed x9, local copies, waits for them, and re-layouts  4.41 us

profile of v2, /device:TPU:1, one launch (start us, length us, event | category | flops | bytes accessed | tf_op | source)
XLA Modules:
  0.0 171.2 jit_solution(6459260554397230139)
XLA Ops:
  0.6 0.0 copy-start
  0.6 1.2 copy-done
  1.9 0.0 copy-start.1
  1.9 1.0 copy-done.1
  2.9 0.0 copy-start.2
  2.9 0.8 copy-done.2
  3.7 0.0 copy-start.3
  3.7 0.7 copy-done.3
  4.4 5.0 %shard_map.67 = (f32[8,8,128]{2,1,0:T(8,128)S(1)}, bf16[1024,128]{1,0:T(8,128)(2,1)S(1)}, bf16[2048,128]{1,0:T(8,128)(2,1)S(1)}, f32[1024,128]{1,0:T(8,128)S(1)}...) custom-call(f32[4]{0:T(128)S(1)} %copy-done.3, ...), custom_call_target="tpu_custom_call" | custom-call | tf_op jit(solution)/shard_map/pallas_call | solution.py:211
  9.4 15.7 %all_to_all.55.parts = f32[8,8,128]{2,1,0:T(8,128)S(1)} all-to-all(f32[8,8,128]{2,1,0:T(8,128)S(1)} %get-tuple-element.24), channel_id=1, replica_groups=mesh['gen'=32,'beam'=8] {'beam'}, dimensions={0} | all-to-all | bytes 65536 | tf_op jit(solution)/shard_map/all_to_all | solution.py:222
  25.1 3.3 %shard_map.68 = (f32[32,16,128]{2,1,0:T(8,128)S(1)}, f32[1024,2048]{1,0:T(8,128)S(1)}) custom-call(f32[4]{0:T(128)S(1)} %copy-done.3, f32[8,8,128]{2,1,0:T(8,128)S(1)} %all_to_all.55.parts, bf16[1024,128]{1,0:T(8,128)(2,1)S(1)} %get-tuple-element.25.summed.kept.gen_emb, bf16[2048,128]{1,0:T(8,128)(2,1)S(1)} %get-tuple-element.26.kept.summed.beam_emb), custom_call_target="tpu_custom_call" | custom-call | tf_op jit(solution)/shard_map/pallas_call | solution.py:211
  28.4 17.9 %all_to_all.56.parts = f32[32,16,128]{2,1,0:T(8,128)S(1)} all-to-all(f32[32,16,128]{2,1,0:T(8,128)S(1)} %get-tuple-element.27), channel_id=1, replica_groups=mesh['gen'=32,'beam'=8] {'gen'}, dimensions={0} | all-to-all | bytes 524288 | tf_op jit(solution)/shard_map/all_to_all | solution.py:222
  46.3 3.2 %shard_map.69 = (f32[8,8,128]{2,1,0:T(8,128)S(1)}, f32[2048,1024]{1,0:T(8,128)S(1)}) custom-call(f32[4]{0:T(128)S(1)} %copy-done.3, f32[32,16,128]{2,1,0:T(8,128)S(1)} %all_to_all.56.parts, bf16[2048,128]{1,0:T(8,128)(2,1)S(1)} %get-tuple-element.26.kept.summed.beam_emb, bf16[1024,128]{1,0:T(8,128)(2,1)S(1)} %get-tuple-element.25.summed.kept.gen_emb), custom_call_target="tpu_custom_call" | custom-call | tf_op jit(solution)/shard_map/pallas_call | solution.py:211
  49.4 9.2 %all_to_all.57.parts = f32[8,8,128]{2,1,0:T(8,128)S(1)} all-to-all(f32[8,8,128]{2,1,0:T(8,128)S(1)} %get-tuple-element.28), channel_id=1, replica_groups=mesh['gen'=32,'beam'=8] {'beam'}, dimensions={0} | all-to-all | bytes 65536 | tf_op jit(solution)/shard_map/all_to_all | solution.py:222
  58.7 2.9 %shard_map.70 = f32[32,16,128]{2,1,0:T(8,128)S(1)} custom-call(f32[4]{0:T(128)S(1)} %copy-done.3, f32[8,8,128]{2,1,0:T(8,128)S(1)} %all_to_all.57.parts, f32[1024,2048]{1,0:T(8,128)S(1)} %get-tuple-element.29.cross), custom_call_target="tpu_custom_call" | custom-call | tf_op jit(solution)/shard_map/pallas_call | solution.py:211
  61.6 13.6 %all_to_all.58.parts = f32[32,16,128]{2,1,0:T(8,128)S(1)} all-to-all(f32[32,16,128]{2,1,0:T(8,128)S(1)} %shard_map.70), channel_id=1, replica_groups=mesh['gen'=32,'beam'=8] {'gen'}, dimensions={0} | all-to-all | bytes 524288 | tf_op jit(solution)/shard_map/all_to_all | solution.py:222
  75.2 2.8 %shard_map.71 = f32[8,8,128]{2,1,0:T(8,128)S(1)} custom-call(f32[4]{0:T(128)S(1)} %copy-done.3, f32[32,16,128]{2,1,0:T(8,128)S(1)} %all_to_all.58.parts, f32[2048,1024]{1,0:T(8,128)S(1)} %get-tuple-element.30.cross), custom_call_target="tpu_custom_call" | custom-call | tf_op jit(solution)/shard_map/pallas_call | solution.py:211
  78.1 9.2 %all_to_all.59.parts = f32[8,8,128]{2,1,0:T(8,128)S(1)} all-to-all(f32[8,8,128]{2,1,0:T(8,128)S(1)} %shard_map.71), channel_id=1, replica_groups=mesh['gen'=32,'beam'=8] {'beam'}, dimensions={0} | all-to-all | bytes 65536 | tf_op jit(solution)/shard_map/all_to_all | solution.py:222
  87.3 2.9 %shard_map.72 = f32[32,16,128]{2,1,0:T(8,128)S(1)} custom-call(f32[4]{0:T(128)S(1)} %copy-done.3, f32[8,8,128]{2,1,0:T(8,128)S(1)} %all_to_all.59.parts, f32[1024,2048]{1,0:T(8,128)S(1)} %get-tuple-element.29.cross), custom_call_target="tpu_custom_call" | custom-call | tf_op jit(solution)/shard_map/pallas_call | solution.py:211
  90.3 13.6 %all_to_all.60.parts = f32[32,16,128]{2,1,0:T(8,128)S(1)} all-to-all(f32[32,16,128]{2,1,0:T(8,128)S(1)} %shard_map.72), channel_id=1, replica_groups=mesh['gen'=32,'beam'=8] {'gen'}, dimensions={0} | all-to-all | bytes 524288 | tf_op jit(solution)/shard_map/all_to_all | solution.py:222
  103.9 2.8 %shard_map.73 = f32[8,8,128]{2,1,0:T(8,128)S(1)} custom-call(f32[4]{0:T(128)S(1)} %copy-done.3, f32[32,16,128]{2,1,0:T(8,128)S(1)} %all_to_all.60.parts, f32[2048,1024]{1,0:T(8,128)S(1)} %get-tuple-element.30.cross), custom_call_target="tpu_custom_call" | custom-call | tf_op jit(solution)/shard_map/pallas_call | solution.py:211
  106.7 9.2 %all_to_all.61.parts.gen_parts = f32[8,8,128]{2,1,0:T(8,128)S(1)} all-to-all(f32[8,8,128]{2,1,0:T(8,128)S(1)} %shard_map.73), channel_id=1, replica_groups=mesh['gen'=32,'beam'=8] {'beam'}, dimensions={0} | all-to-all | bytes 65536 | tf_op jit(solution)/shard_map/all_to_all | solution.py:222
  116.0 2.8 %shard_map.74 = (f32[32,16,128]{2,1,0:T(8,128)S(1)}, f32[1024,2048]{1,0:T(8,128)S(1)}, f32[32,128]{1,0:T(8,128)S(1)}) custom-call(f32[4]{0:T(128)S(1)} %copy-done.3, f32[8,8,128]{2,1,0:T(8,128)S(1)} %all_to_all.61.parts.gen_parts, f32[1024,2048]{1,0:T(8,128)S(1)} %get-tuple-element.29.cross), custom_call_target="tpu_custom_call" | custom-call | tf_op jit(solution)/shard_map/pallas_call | solution.py:211
  118.8 13.6 %all_to_all.62.parts = f32[32,16,128]{2,1,0:T(8,128)S(1)} all-to-all(f32[32,16,128]{2,1,0:T(8,128)S(1)} %get-tuple-element.31), channel_id=1, replica_groups=mesh['gen'=32,'beam'=8] {'gen'}, dimensions={0} | all-to-all | bytes 524288 | tf_op jit(solution)/shard_map/all_to_all | solution.py:222
  132.4 5.2 %shard_map.75 = (f32[8,128]{1,0:T(8,128)}, f32[16,128]{1,0:T(8,128)}, f32[256,128]{1,0:T(8,128)S(1)}) custom-call(f32[4]{0:T(128)S(1)} %copy-done.3, f32[32,16,128]{2,1,0:T(8,128)S(1)} %all_to_all.62.parts, f32[8,8,128]{2,1,0:T(8,128)S(1)} %all_to_all.61.parts.gen_parts, f32[1024,2048]{1,0:T(8,128)S(1)} %get-tuple-element.32.kernel, ...), custom_call_target="tpu_custom_call" | custom-call | tf_op jit(solution)/shard_map/pallas_call | solution.py:211
  137.6 11.2 %all_to_all.63 = f32[32,8,128]{2,1,0:T(8,128)S(1)} all-to-all(f32[32,8,128]{2,1,0:T(8,128)S(1)} %bitcast.4), channel_id=1, replica_groups=mesh['gen'=32,'beam'=8] {'gen'}, dimensions={0} | all-to-all | bytes 262144 | tf_op jit(solution)/shard_map/all_to_all | solution.py:222
  148.8 9.2 %all_to_all.64 = f32[8,8,128]{2,1,0:T(8,128)S(1)} all-to-all(f32[8,8,128]{2,1,0:T(8,128)S(1)} %broadcast_in_dim.4), channel_id=1, replica_groups=mesh['gen'=32,'beam'=8] {'beam'}, dimensions={0} | all-to-all | bytes 65536 | tf_op jit(solution)/shard_map/all_to_all | solution.py:222
  158.1 12.4 %all_to_all.65 = f32[32,8,128]{2,1,0:T(8,128)S(1)} all-to-all(f32[32,8,128]{2,1,0:T(8,128)S(1)} %broadcast_in_dim.5), channel_id=1, replica_groups=mesh['gen'=32,'beam'=8] {'gen'}, dimensions={0} | all-to-all | bytes 262144 | tf_op jit(solution)/shard_map/all_to_all | solution.py:222
  170.5 0.7 copy.8
  (4 shorter events, 0.1 us)
Async XLA Ops:
  0.6 1.2 copy-start
  1.9 1.0 copy-start.1
  2.9 0.8 copy-start.2
  3.7 0.7 copy-start.3

commit v3 on v2

v3 whole, which is shorter than its diff:
```python
import functools
import math

import jax
import jax.numpy as jnp
from jax import lax
from jax.experimental import pallas as pl
from jax.experimental.pallas import tpu as pltpu
from jax.sharding import PartitionSpec as P

SWEEPS = 4
LOG2E = 1.4426950408889634
BYTES = 16 * 1024 * 1024
FIRST_BYTES = 20 * 1024 * 1024
NT = (((1,), (1,)), ((), ()))
F32 = jnp.float32
BF16 = jnp.bfloat16
WIDE = 256
BLOCK = 64
DEEP = 512


def of_sweep(table, sweep):
    return table[sweep : sweep + 1, :], table[SWEEPS + sweep : SWEEPS + sweep + 1, :]


def tabled(eps, table):
    for sweep in range(SWEEPS):
        e = jnp.broadcast_to(eps[:, sweep : sweep + 1], (1, 128))
        table[sweep : sweep + 1, :] = e
        table[SWEEPS + sweep : SWEEPS + sweep + 1, :] = 2.0 * LOG2E / e


def merged(parts, e, scale):
    count = parts.shape[0]
    top = parts[0]
    for d in range(1, count):
        top = jnp.maximum(top, parts[d])
    total = jnp.exp2((parts[0] - top) * scale)
    for d in range(1, count):
        total = total + jnp.exp2((parts[d] - top) * scale)
    return top + jnp.log2(total) * (e * (0.5 / LOG2E))


def spread(dense, column):
    turned = jnp.transpose(dense)
    for r in range(dense.shape[0]):
        column[r * 128 : (r + 1) * 128, :] = jnp.broadcast_to(turned[:, r : r + 1], (128, 128))


def partial_lse(cross, column, table, sweep, top_scr, sum_scr, out, factors=None, kernel=None):
    rows, lanes = cross.shape
    count, tiles = lanes // WIDE, WIDE // 128
    e, scale = of_sweep(table, sweep)
    wide_scale = jnp.concatenate([scale] * tiles, axis=1)

    def lift(r):
        return jnp.concatenate([column[r : r + BLOCK, :]] * tiles, axis=1)

    def fold(x, op):
        return op(x.reshape(BLOCK // 8, 8, WIDE), axis=0)

    def put(scr, n, line):
        for i in range(tiles):
            scr[n * tiles + i : n * tiles + i + 1, :] = line[:, i * 128 : (i + 1) * 128]

    last = None
    for n in range(count + 1):
        new, old = slice(n * WIDE, (n + 1) * WIDE), slice((n - 1) * WIDE, n * WIDE)
        top = total = None
        for r in range(0, rows, BLOCK):
            at = slice(r, r + BLOCK)
            if n < count:
                if factors is None:
                    t = cross[at, new]
                else:
                    if r % DEEP == 0:
                        summed, kept = factors
                        made = lax.dot_general(summed[r : r + DEEP, :], kept[new, :], NT, preferred_element_type=F32)
                    t = made[r % DEEP : r % DEEP + BLOCK]
                    cross[at, new] = t
                t = fold(t + lift(r), jnp.max)
                top = t if top is None else jnp.maximum(top, t)
            if n > 0:
                p = jnp.exp2((cross[at, old] + lift(r) - last) * wide_scale)
                if kernel is not None:
                    kernel[at, old] = p
                p = fold(p, jnp.sum)
                total = p if total is None else total + p
        if n > 0:
            put(sum_scr, n - 1, jnp.sum(total, axis=0, keepdims=True))
        if n < count:
            last = jnp.max(top, axis=0, keepdims=True)
            put(top_scr, n, last)
    part = top_scr[...] + jnp.log2(sum_scr[...]) * (e * (0.5 / LOG2E))
    out[...] = jnp.broadcast_to(part[None], out.shape)


def embed(showers, weight):
    return jnp.tanh(jnp.dot(showers[...], weight[...], preferred_element_type=F32))


def first_kernel(
    eps_far, gen_far, beam_far, weight_far, out, gen_emb, beam_emb, table,
    column, top_scr, sum_scr, cross, eps, gen_showers, beam_showers, weight, sems,
):
    pairs = ((weight_far, weight), (beam_far, beam_showers), (gen_far, gen_showers), (eps_far, eps))
    copies = [pltpu.make_async_copy(src, dst, sems.at[i]) for i, (src, dst) in enumerate(pairs)]
    for copy in copies:
        copy.start()
    copies[0].wait()
    copies[1].wait()
    beam = embed(beam_showers, weight).astype(BF16)
    beam_emb[...] = beam
    beam = beam.astype(F32)
    column[...] = jnp.broadcast_to(-0.5 * jnp.sum(beam * beam, axis=1, keepdims=True), column.shape)
    copies[2].wait()
    gen_emb[...] = embed(gen_showers, weight).astype(BF16)
    copies[3].wait()
    tabled(eps, table)
    partial_lse(cross, column, table, 0, top_scr, sum_scr, out, (beam_emb, gen_emb))


def made_kernel(before, now, log_count, table, parts, summed, kept, out, cross, column, top_scr, sum_scr):
    e, scale = of_sweep(table, before)
    spread(e * (0.5 * log_count) - merged(parts, e, scale), column)
    partial_lse(cross, column, table, now, top_scr, sum_scr, out, (summed, kept))


def pass_kernel(before, now, log_count, table, parts, cross, out, column, top_scr, sum_scr):
    e, scale = of_sweep(table, before)
    spread(e * (0.5 * log_count) - merged(parts, e, scale), column)
    partial_lse(cross, column, table, now, top_scr, sum_scr, out)


def kept_kernel(before, now, log_count, table, parts, cross, out, kernel, stats, column):
    e, scale = of_sweep(table, before)
    spread(e * (0.5 * log_count) - merged(parts, e, scale), column)
    half = stats.shape[0] // 2
    tops, sums = stats.at[pl.ds(0, half)], stats.at[pl.ds(half, half)]
    partial_lse(cross, column, table, now, tops, sums, out, None, kernel)


def halves(x):
    one = x.astype(BF16)
    return jnp.concatenate([one, (x - one.astype(F32)).astype(BF16)], axis=0)


def last_kernel(
    log_gen, log_beam, table, parts, gen_parts, kernel, stats, gen_emb, beam_emb, gen_showers, beam_showers, weight,
    gen_pot, beam_pot, grad, rows_scr, moved_scr, gen_t, pre_t,
):
    e, scale = of_sweep(table, SWEEPS - 1)
    beam_half = e * (0.5 * log_gen) - merged(parts, e, scale)
    gen_half = e * (0.5 * log_beam) - merged(gen_parts, e, scale)
    count = stats.shape[0] // 2
    factor = jnp.exp2((stats[:count, :] + beam_half) * scale - log_beam * LOG2E)
    col_mass = stats[count:, :] * factor
    tiles = WIDE // 128

    def line(dense, n):
        return jnp.concatenate([dense[n * tiles + i : n * tiles + i + 1, :] for i in range(tiles)], axis=1)

    def square(turned):
        turned = turned.astype(F32)
        return jnp.sum(turned * turned, axis=0, keepdims=True)

    for r in range(gen_half.shape[0]):
        at = slice(r * 128, (r + 1) * 128)
        turned = jnp.transpose(gen_emb[at, :])
        gen_t[:, at] = turned
        gen_pot[r : r + 1, :] = 2.0 * gen_half[r : r + 1, :] + square(turned)

    total = None
    for n in range(kernel.shape[1] // WIDE):
        at = slice(n * WIDE, (n + 1) * WIDE)
        mass = kernel[:, at] * line(factor, n)
        plan = mass.astype(BF16)
        sums = mass[:, :128]
        for i in range(1, tiles):
            sums = sums + mass[:, i * 128 : (i + 1) * 128]
        moved = jnp.dot(plan, beam_emb[at, :], preferred_element_type=F32)
        if n == 0:
            rows_scr[...] = sums
            moved_scr[...] = moved
        else:
            rows_scr[...] += sums
            moved_scr[...] += moved
        moved = jnp.dot(gen_t[...], plan, preferred_element_type=F32)
        act = jnp.tanh(
            lax.dot_general(weight[...], beam_showers[at, :], (((0,), (1,)), ((), ())), preferred_element_type=F32)
        )
        beam_t = act.astype(BF16)
        for i in range(tiles):
            t = n * tiles + i
            beam_pot[t : t + 1, :] = 2.0 * beam_half[t : t + 1, :] + square(beam_t[:, i * 128 : (i + 1) * 128])
        pre = 2.0 * (line(col_mass, n) * beam_t.astype(F32) - moved) * (1.0 - act * act)
        part = jnp.dot(halves(pre), beam_showers[at, :], preferred_element_type=F32)
        total = part if total is None else total + part
    row_mass = jnp.sum(rows_scr[...], axis=1, keepdims=True)
    act = embed(gen_showers, weight)
    pre = 2.0 * (row_mass * gen_emb[...].astype(F32) - moved_scr[...]) * (1.0 - act * act)
    for r in range(gen_half.shape[0]):
        at = slice(r * 128, (r + 1) * 128)
        pre_t[:, at] = jnp.transpose(pre[at, :])
    total = total + jnp.dot(halves(pre_t[...]), gen_showers[...], preferred_element_type=F32)
    width = total.shape[0] // 2
    grad[...] = jnp.transpose(total[:width] + total[width:])


LOCAL = pl.BlockSpec(memory_space=pltpu.VMEM)
FAR = pl.BlockSpec(memory_space=pltpu.HBM)


def call(kernel, operands, outs, scratch=(), far=(), sems=0, limit=BYTES):
    specs = [FAR if i in far else LOCAL for i in range(len(operands))]
    scratch = [pltpu.VMEM(*s) for s in scratch]
    if sems:
        scratch.append(pltpu.SemaphoreType.DMA((sems,)))
    return pl.pallas_call(
        kernel,
        out_shape=tuple(jax.ShapeDtypeStruct(*o) for o in outs),
        in_specs=specs,
        out_specs=tuple(LOCAL for _ in outs),
        scratch_shapes=scratch,
        compiler_params=pltpu.CompilerParams(vmem_limit_bytes=limit),
    )(*operands)


def swap(x, axis):
    return lax.all_to_all(x, axis, split_axis=0, concat_axis=0, tiled=True)


def on_device(gen_showers, beam_showers, embed_weight, eps_roster):
    eps_roster = eps_roster.reshape(1, SWEEPS)
    gens, beams = lax.axis_size("gen"), lax.axis_size("beam")
    rows, columns = gen_showers.shape[0], beam_showers.shape[0]
    depth, width = embed_weight.shape
    log_gen, log_beam = math.log(rows * gens), math.log(columns * beams)
    r, c = rows // 128, columns // 128
    gen_out, beam_out = ((beams, r, 128), F32), ((gens, c, 128), F32)
    gen_scratch = [((columns, 128), F32), ((r, 128), F32), ((r, 128), F32)]
    beam_scratch = [((rows, 128), F32), ((c, 128), F32), ((c, 128), F32)]
    gen_parts, gen_emb, beam_emb, table = call(
        first_kernel,
        (eps_roster, gen_showers, beam_showers, embed_weight),
        [gen_out, ((rows, width), BF16), ((columns, width), BF16), ((2 * SWEEPS, 128), F32)],
        gen_scratch
        + [((columns, rows), F32), (eps_roster.shape, F32)]
        + [(a.shape, BF16) for a in (gen_showers, beam_showers, embed_weight)],
        far=(0, 1, 2, 3),
        sems=4,
        limit=FIRST_BYTES,
    )
    gen_parts = swap(gen_parts, "beam")
    beam_parts, cross = call(
        functools.partial(made_kernel, 0, 0, log_beam),
        (table, gen_parts, gen_emb, beam_emb),
        [beam_out, ((rows, columns), F32)],
        beam_scratch,
    )
    for sweep in range(1, SWEEPS):
        beam_parts = swap(beam_parts, "gen")
        if sweep == 1:
            gen_parts, turned_cross = call(
                functools.partial(made_kernel, sweep - 1, sweep, log_gen),
                (table, beam_parts, beam_emb, gen_emb),
                [gen_out, ((columns, rows), F32)],
                gen_scratch,
            )
        else:
            (gen_parts,) = call(
                functools.partial(pass_kernel, sweep - 1, sweep, log_gen),
                (table, beam_parts, turned_cross),
                [gen_out],
                gen_scratch,
            )
        gen_parts = swap(gen_parts, "beam")
        if sweep < SWEEPS - 1:
            (beam_parts,) = call(
                functools.partial(pass_kernel, sweep, sweep, log_beam),
                (table, gen_parts, cross),
                [beam_out],
                beam_scratch,
            )
        else:
            beam_parts, kernel, stats = call(
                functools.partial(kept_kernel, sweep, sweep, log_beam),
                (table, gen_parts, cross),
                [beam_out, ((rows, columns), F32), ((2 * c, 128), F32)],
                beam_scratch[:1],
            )
    beam_parts = swap(beam_parts, "gen")
    gen_pot, beam_pot, grad = call(
        functools.partial(last_kernel, log_gen, log_beam),
        (
            table, beam_parts, gen_parts, kernel, stats, gen_emb, beam_emb, gen_showers, beam_showers, embed_weight,
        ),
        [((r, 128), F32), ((c, 128), F32), ((depth, width), F32)],
        [((rows, 128), F32), ((rows, width), F32), ((width, rows), BF16), ((width, rows), F32)],
    )
    piece = swap(grad.reshape(gens, depth // gens, width), "gen").sum(0)
    piece = swap(jnp.broadcast_to(piece[None], (beams,) + piece.shape), "beam").sum(0)
    grad = swap(jnp.broadcast_to(piece[None], (gens,) + piece.shape), "gen")
    return gen_pot.reshape(rows), beam_pot.reshape(columns), grad.reshape(depth, width)


def solution(mesh):
    in_specs = (P("gen", None), P("beam", None), P(), P())
    out_specs = (P("gen"), P("beam"), P())
    return jax.shard_map(on_device, mesh=mesh, in_specs=in_specs, out_specs=out_specs, check_vma=False)
```

time: 172 us -> 165 us (0.959)
  Pallas kernels: 31 us -> 23.9 us
    pallas_call x9, Pallas kernels: 31 us -> 23.9 us  [call(): pl.pallas_call(kernel, out_shape=tuple((jax.ShapeDtypeStruct(*o) for o in...]
    unnamed x9 -> x11, local copies, waits for them, and re-layouts: 4.41 us -> 4.41 us
where the time goes in v3:
time: 165 us; the launch traced here: 164 us
  blocking collectives  135 us (82%)
  Pallas kernels  23.9 us (14%)
  local copies, waits for them, and re-layouts  4.43 us (3%)
    all_to_all x11, blocking collectives, swap(): return lax.all_to_all(x, axis, split_axis=0, concat_axis=0, tiled=True)  135 us
    pallas_call x9, Pallas kernels, call(): pl.pallas_call(kernel, out_shape=tuple((jax.ShapeDtypeStruct(*o) for o in...  23.9 us
    unnamed x11, local copies, waits for them, and re-layouts  4.41 us

profile of v3, /device:TPU:1, one launch (start us, length us, event | category | flops | bytes accessed | tf_op | source)
XLA Modules:
  0.0 164.1 jit_solution(1627120970521799256)
XLA Ops:
  0.6 0.0 copy-start
  0.6 1.2 copy-done
  1.9 0.0 copy-start.1
  1.9 1.0 copy-done.1
  2.9 0.0 copy-start.2
  2.9 0.8 copy-done.2
  3.7 0.0 copy-start.4
  3.7 0.7 copy-done.4
  4.4 4.2 %shard_map.67 = (f32[8,8,128]{2,1,0:T(8,128)S(1)}, bf16[1024,128]{1,0:T(8,128)(2,1)S(1)}, bf16[2048,128]{1,0:T(8,128)(2,1)S(1)}, f32[8,128]{1,0:T(8,128)S(1)}) custom-call(f32[1,4]{1,0:T(1,128)S(1)} %bitcast.6, bf16[1024,256]{1,0:T(8,128)(2,1)S(1)} %copy-done.1, bf16[2048,256]{1,0:T(8,128)(2,1)S(1)} %copy-done, bf16[256,128]{1,0:T(8,128)(2,1)S(1)} %copy-done.2), custom_call_target="tpu_custom_call" | custom-call | tf_op jit(solution)/shard_map/pallas_call | solution.py:220
  8.6 15.7 %all_to_all.55.parts = f32[8,8,128]{2,1,0:T(8,128)S(1)} all-to-all(f32[8,8,128]{2,1,0:T(8,128)S(1)} %get-tuple-element.18), channel_id=1, replica_groups=mesh['gen'=32,'beam'=8] {'beam'}, dimensions={0} | all-to-all | bytes 65536 | tf_op jit(solution)/shard_map/all_to_all | solution.py:231
  24.3 2.7 %shard_map.68 = (f32[32,16,128]{2,1,0:T(8,128)S(1)}, f32[1024,2048]{1,0:T(8,128)S(1)}) custom-call(f32[8,128]{1,0:T(8,128)S(1)} %get-tuple-element.17.table, f32[8,8,128]{2,1,0:T(8,128)S(1)} %all_to_all.55.parts, bf16[1024,128]{1,0:T(8,128)(2,1)S(1)} %get-tuple-element.19.summed.kept.gen_emb, bf16[2048,128]{1,0:T(8,128)(2,1)S(1)} %get-tuple-element.20.kept.summed.beam_emb), custom_call_target="tpu_custom_call" | custom-call | tf_op jit(solution)/shard_map/pallas_call | solution.py:220
  27.0 17.9 %all_to_all.56.parts = f32[32,16,128]{2,1,0:T(8,128)S(1)} all-to-all(f32[32,16,128]{2,1,0:T(8,128)S(1)} %get-tuple-element.21), channel_id=1, replica_groups=mesh['gen'=32,'beam'=8] {'gen'}, dimensions={0} | all-to-all | bytes 524288 | tf_op jit(solution)/shard_map/all_to_all | solution.py:231
  44.9 2.7 %shard_map.69 = (f32[8,8,128]{2,1,0:T(8,128)S(1)}, f32[2048,1024]{1,0:T(8,128)S(1)}) custom-call(f32[8,128]{1,0:T(8,128)S(1)} %get-tuple-element.17.table, f32[32,16,128]{2,1,0:T(8,128)S(1)} %all_to_all.56.parts, bf16[2048,128]{1,0:T(8,128)(2,1)S(1)} %get-tuple-element.20.kept.summed.beam_emb, bf16[1024,128]{1,0:T(8,128)(2,1)S(1)} %get-tuple-element.19.summed.kept.gen_emb), custom_call_target="tpu_custom_call" | custom-call | tf_op jit(solution)/shard_map/pallas_call | solution.py:220
  47.6 9.2 %all_to_all.57.parts = f32[8,8,128]{2,1,0:T(8,128)S(1)} all-to-all(f32[8,8,128]{2,1,0:T(8,128)S(1)} %get-tuple-element.22), channel_id=1, replica_groups=mesh['gen'=32,'beam'=8] {'beam'}, dimensions={0} | all-to-all | bytes 65536 | tf_op jit(solution)/shard_map/all_to_all | solution.py:231
  56.9 2.0 %shard_map.70 = f32[32,16,128]{2,1,0:T(8,128)S(1)} custom-call(f32[8,128]{1,0:T(8,128)S(1)} %get-tuple-element.17.table, f32[8,8,128]{2,1,0:T(8,128)S(1)} %all_to_all.57.parts, f32[1024,2048]{1,0:T(8,128)S(1)} %get-tuple-element.23.cross), custom_call_target="tpu_custom_call" | custom-call | tf_op jit(solution)/shard_map/pallas_call | solution.py:220
  58.9 13.6 %all_to_all.58.parts = f32[32,16,128]{2,1,0:T(8,128)S(1)} all-to-all(f32[32,16,128]{2,1,0:T(8,128)S(1)} %shard_map.70), channel_id=1, replica_groups=mesh['gen'=32,'beam'=8] {'gen'}, dimensions={0} | all-to-all | bytes 524288 | tf_op jit(solution)/shard_map/all_to_all | solution.py:231
  72.6 2.0 %shard_map.71 = f32[8,8,128]{2,1,0:T(8,128)S(1)} custom-call(f32[8,128]{1,0:T(8,128)S(1)} %get-tuple-element.17.table, f32[32,16,128]{2,1,0:T(8,128)S(1)} %all_to_all.58.parts, f32[2048,1024]{1,0:T(8,128)S(1)} %get-tuple-element.24.cross), custom_call_target="tpu_custom_call" | custom-call | tf_op jit(solution)/shard_map/pallas_call | solution.py:220
  74.6 9.2 %all_to_all.59.parts = f32[8,8,128]{2,1,0:T(8,128)S(1)} all-to-all(f32[8,8,128]{2,1,0:T(8,128)S(1)} %shard_map.71), channel_id=1, replica_groups=mesh['gen'=32,'beam'=8] {'beam'}, dimensions={0} | all-to-all | bytes 65536 | tf_op jit(solution)/shard_map/all_to_all | solution.py:231
  83.8 2.0 %shard_map.72 = f32[32,16,128]{2,1,0:T(8,128)S(1)} custom-call(f32[8,128]{1,0:T(8,128)S(1)} %get-tuple-element.17.table, f32[8,8,128]{2,1,0:T(8,128)S(1)} %all_to_all.59.parts, f32[1024,2048]{1,0:T(8,128)S(1)} %get-tuple-element.23.cross), custom_call_target="tpu_custom_call" | custom-call | tf_op jit(solution)/shard_map/pallas_call | solution.py:220
  85.9 13.6 %all_to_all.60.parts = f32[32,16,128]{2,1,0:T(8,128)S(1)} all-to-all(f32[32,16,128]{2,1,0:T(8,128)S(1)} %shard_map.72), channel_id=1, replica_groups=mesh['gen'=32,'beam'=8] {'gen'}, dimensions={0} | all-to-all | bytes 524288 | tf_op jit(solution)/shard_map/all_to_all | solution.py:231
  99.5 0.0 copy-start.3
  99.5 2.0 %shard_map.73 = f32[8,8,128]{2,1,0:T(8,128)S(1)} custom-call(f32[8,128]{1,0:T(8,128)S(1)} %get-tuple-element.17.table, f32[32,16,128]{2,1,0:T(8,128)S(1)} %all_to_all.60.parts, f32[2048,1024]{1,0:T(8,128)S(1)} %get-tuple-element.24.cross), custom_call_target="tpu_custom_call" | custom-call | tf_op jit(solution)/shard_map/pallas_call | solution.py:220
  101.5 9.2 %all_to_all.61.parts.gen_parts = f32[8,8,128]{2,1,0:T(8,128)S(1)} all-to-all(f32[8,8,128]{2,1,0:T(8,128)S(1)} %shard_map.73), channel_id=1, replica_groups=mesh['gen'=32,'beam'=8] {'beam'}, dimensions={0} | all-to-all | bytes 65536 | tf_op jit(solution)/shard_map/all_to_all | solution.py:231
  110.7 2.0 %shard_map.74 = (f32[32,16,128]{2,1,0:T(8,128)S(1)}, f32[1024,2048]{1,0:T(8,128)S(1)}, f32[32,128]{1,0:T(8,128)S(1)}) custom-call(f32[8,128]{1,0:T(8,128)S(1)} %get-tuple-element.17.table, f32[8,8,128]{2,1,0:T(8,128)S(1)} %all_to_all.61.parts.gen_parts, f32[1024,2048]{1,0:T(8,128)S(1)} %get-tuple-element.23.cross), custom_call_target="tpu_custom_call" | custom-call | tf_op jit(solution)/shard_map/pallas_call | solution.py:220
  112.8 13.6 %all_to_all.62.parts = f32[32,16,128]{2,1,0:T(8,128)S(1)} all-to-all(f32[32,16,128]{2,1,0:T(8,128)S(1)} %get-tuple-element.25), channel_id=1, replica_groups=mesh['gen'=32,'beam'=8] {'gen'}, dimensions={0} | all-to-all | bytes 524288 | tf_op jit(solution)/shard_map/all_to_all | solution.py:231
  126.4 0.0 copy-done.3
  126.4 4.1 %shard_map.75 = (f32[8,128]{1,0:T(8,128)}, f32[16,128]{1,0:T(8,128)}, f32[256,128]{1,0:T(8,128)S(1)}) custom-call(f32[8,128]{1,0:T(8,128)S(1)} %get-tuple-element.17.table, f32[32,16,128]{2,1,0:T(8,128)S(1)} %all_to_all.62.parts, f32[8,8,128]{2,1,0:T(8,128)S(1)} %all_to_all.61.parts.gen_parts, f32[1024,2048]{1,0:T(8,128)S(1)} %get-tuple-element.26.kernel, ...), custom_call_target="tpu_custom_call" | custom-call | tf_op jit(solution)/shard_map/pallas_call | solution.py:220
  130.5 11.2 %all_to_all.63 = f32[32,8,128]{2,1,0:T(8,128)S(1)} all-to-all(f32[32,8,128]{2,1,0:T(8,128)S(1)} %bitcast.5), channel_id=1, replica_groups=mesh['gen'=32,'beam'=8] {'gen'}, dimensions={0} | all-to-all | bytes 262144 | tf_op jit(solution)/shard_map/all_to_all | solution.py:231
  141.7 9.2 %all_to_all.64 = f32[8,8,128]{2,1,0:T(8,128)S(1)} all-to-all(f32[8,8,128]{2,1,0:T(8,128)S(1)} %broadcast_in_dim.4), channel_id=1, replica_groups=mesh['gen'=32,'beam'=8] {'beam'}, dimensions={0} | all-to-all | bytes 65536 | tf_op jit(solution)/shard_map/all_to_all | solution.py:231
  151.0 12.4 %all_to_all.65 = f32[32,8,128]{2,1,0:T(8,128)S(1)} all-to-all(f32[32,8,128]{2,1,0:T(8,128)S(1)} %broadcast_in_dim.5), channel_id=1, replica_groups=mesh['gen'=32,'beam'=8] {'gen'}, dimensions={0} | all-to-all | bytes 262144 | tf_op jit(solution)/shard_map/all_to_all | solution.py:231
  163.4 0.7 copy.8
  (4 shorter events, 0.1 us)
Async XLA Ops:
  0.6 1.2 copy-start
  1.9 1.0 copy-start.1
  2.9 0.8 copy-start.2
  3.7 0.7 copy-start.4
  99.5 26.9 %copy-start.3 = (bf16[256,128]{1,0:T(8,128)(2,1)S(1)}, bf16[256,128]{1,0:T(8,128)(2,1)}, u32[]{:S(2)}) copy-start(bf16[256,128]{1,0:T(8,128)(2,1)} %weight.1) | copy-start | bytes 196612

commit v4 on v3

--- a/solution.py
+++ b/solution.py
@@ -11,7 +11,7 @@
 SWEEPS = 4
 LOG2E = 1.4426950408889634
 BYTES = 16 * 1024 * 1024
-FIRST_BYTES = 20 * 1024 * 1024
+FIRST_BYTES = 53 * 1024 * 1024
 NT = (((1,), (1,)), ((), ()))
 F32 = jnp.float32
 BF16 = jnp.bfloat16

time: 165 us -> 163 us (0.988)
  local copies, waits for them, and re-layouts: 4.43 us -> 2.17 us
    unnamed x11 -> x9, local copies, waits for them, and re-layouts: 4.41 us -> 2.15 us
where the time goes in v4:
time: 163 us
  blocking collectives  135 us (83%)
  Pallas kernels  25 us (15%)
  local copies, waits for them, and re-layouts  2.17 us (1%)
    all_to_all x11, blocking collectives, swap(): return lax.all_to_all(x, axis, split_axis=0, concat_axis=0, tiled=True)  135 us
    pallas_call x9, Pallas kernels, call(): pl.pallas_call(kernel, out_shape=tuple((jax.ShapeDtypeStruct(*o) for o in...  25 us

profile of v4, /device:TPU:1, one launch (start us, length us, event | category | flops | bytes accessed | tf_op | source)
XLA Modules:
  0.0 162.9 jit_solution(14420878422049691837)
XLA Ops:
  0.6 0.0 copy-start.2
  0.6 0.8 copy-done.2
  1.5 0.0 copy-start.3
  1.5 0.7 copy-done.3
  2.1 5.3 %shard_map.67 = (f32[8,8,128]{2,1,0:T(8,128)S(1)}, bf16[1024,128]{1,0:T(8,128)(2,1)S(1)}, bf16[2048,128]{1,0:T(8,128)(2,1)S(1)}, f32[8,128]{1,0:T(8,128)S(1)}) custom-call(f32[1,4]{1,0:T(1,128)S(1)} %bitcast.6, bf16[1024,256]{1,0:T(8,128)(2,1)} %gen_showers.1, bf16[2048,256]{1,0:T(8,128)(2,1)} %beam_showers.1, bf16[256,128]{1,0:T(8,128)(2,1)S(1)} %copy-done.2), custom_call_target="tpu_custom_call" | custom-call | tf_op jit(solution)/shard_map/pallas_call | solution.py:220
  7.4 15.7 %all_to_all.55.parts = f32[8,8,128]{2,1,0:T(8,128)S(1)} all-to-all(f32[8,8,128]{2,1,0:T(8,128)S(1)} %get-tuple-element.18), channel_id=1, replica_groups=mesh['gen'=32,'beam'=8] {'beam'}, dimensions={0} | all-to-all | bytes 65536 | tf_op jit(solution)/shard_map/all_to_all | solution.py:231
  23.1 2.7 %shard_map.68 = (f32[32,16,128]{2,1,0:T(8,128)S(1)}, f32[1024,2048]{1,0:T(8,128)S(1)}) custom-call(f32[8,128]{1,0:T(8,128)S(1)} %get-tuple-element.17.table, f32[8,8,128]{2,1,0:T(8,128)S(1)} %all_to_all.55.parts, bf16[1024,128]{1,0:T(8,128)(2,1)S(1)} %get-tuple-element.19.summed.kept.gen_emb, bf16[2048,128]{1,0:T(8,128)(2,1)S(1)} %get-tuple-element.20.kept.summed.beam_emb), custom_call_target="tpu_custom_call" | custom-call | tf_op jit(solution)/shard_map/pallas_call | solution.py:220
  25.9 17.9 %all_to_all.56.parts = f32[32,16,128]{2,1,0:T(8,128)S(1)} all-to-all(f32[32,16,128]{2,1,0:T(8,128)S(1)} %get-tuple-element.21), channel_id=1, replica_groups=mesh['gen'=32,'beam'=8] {'gen'}, dimensions={0} | all-to-all | bytes 524288 | tf_op jit(solution)/shard_map/all_to_all | solution.py:231
  43.8 2.7 %shard_map.69 = (f32[8,8,128]{2,1,0:T(8,128)S(1)}, f32[2048,1024]{1,0:T(8,128)S(1)}) custom-call(f32[8,128]{1,0:T(8,128)S(1)} %get-tuple-element.17.table, f32[32,16,128]{2,1,0:T(8,128)S(1)} %all_to_all.56.parts, bf16[2048,128]{1,0:T(8,128)(2,1)S(1)} %get-tuple-element.20.kept.summed.beam_emb, bf16[1024,128]{1,0:T(8,128)(2,1)S(1)} %get-tuple-element.19.summed.kept.gen_emb), custom_call_target="tpu_custom_call" | custom-call | tf_op jit(solution)/shard_map/pallas_call | solution.py:220
  46.5 9.2 %all_to_all.57.parts = f32[8,8,128]{2,1,0:T(8,128)S(1)} all-to-all(f32[8,8,128]{2,1,0:T(8,128)S(1)} %get-tuple-element.22), channel_id=1, replica_groups=mesh['gen'=32,'beam'=8] {'beam'}, dimensions={0} | all-to-all | bytes 65536 | tf_op jit(solution)/shard_map/all_to_all | solution.py:231
  55.7 2.0 %shard_map.70 = f32[32,16,128]{2,1,0:T(8,128)S(1)} custom-call(f32[8,128]{1,0:T(8,128)S(1)} %get-tuple-element.17.table, f32[8,8,128]{2,1,0:T(8,128)S(1)} %all_to_all.57.parts, f32[1024,2048]{1,0:T(8,128)S(1)} %get-tuple-element.23.cross), custom_call_target="tpu_custom_call" | custom-call | tf_op jit(solution)/shard_map/pallas_call | solution.py:220
  57.8 13.6 %all_to_all.58.parts = f32[32,16,128]{2,1,0:T(8,128)S(1)} all-to-all(f32[32,16,128]{2,1,0:T(8,128)S(1)} %shard_map.70), channel_id=1, replica_groups=mesh['gen'=32,'beam'=8] {'gen'}, dimensions={0} | all-to-all | bytes 524288 | tf_op jit(solution)/shard_map/all_to_all | solution.py:231
  71.4 2.0 %shard_map.71 = f32[8,8,128]{2,1,0:T(8,128)S(1)} custom-call(f32[8,128]{1,0:T(8,128)S(1)} %get-tuple-element.17.table, f32[32,16,128]{2,1,0:T(8,128)S(1)} %all_to_all.58.parts, f32[2048,1024]{1,0:T(8,128)S(1)} %get-tuple-element.24.cross), custom_call_target="tpu_custom_call" | custom-call | tf_op jit(solution)/shard_map/pallas_call | solution.py:220
  73.4 9.2 %all_to_all.59.parts = f32[8,8,128]{2,1,0:T(8,128)S(1)} all-to-all(f32[8,8,128]{2,1,0:T(8,128)S(1)} %shard_map.71), channel_id=1, replica_groups=mesh['gen'=32,'beam'=8] {'beam'}, dimensions={0} | all-to-all | bytes 65536 | tf_op jit(solution)/shard_map/all_to_all | solution.py:231
  82.7 2.0 %shard_map.72 = f32[32,16,128]{2,1,0:T(8,128)S(1)} custom-call(f32[8,128]{1,0:T(8,128)S(1)} %get-tuple-element.17.table, f32[8,8,128]{2,1,0:T(8,128)S(1)} %all_to_all.59.parts, f32[1024,2048]{1,0:T(8,128)S(1)} %get-tuple-element.23.cross), custom_call_target="tpu_custom_call" | custom-call | tf_op jit(solution)/shard_map/pallas_call | solution.py:220
  84.7 13.6 %all_to_all.60.parts = f32[32,16,128]{2,1,0:T(8,128)S(1)} all-to-all(f32[32,16,128]{2,1,0:T(8,128)S(1)} %shard_map.72), channel_id=1, replica_groups=mesh['gen'=32,'beam'=8] {'gen'}, dimensions={0} | all-to-all | bytes 524288 | tf_op jit(solution)/shard_map/all_to_all | solution.py:231
  98.3 0.0 copy-start
  98.3 0.0 copy-start.1
  98.3 2.0 %shard_map.73 = f32[8,8,128]{2,1,0:T(8,128)S(1)} custom-call(f32[8,128]{1,0:T(8,128)S(1)} %get-tuple-element.17.table, f32[32,16,128]{2,1,0:T(8,128)S(1)} %all_to_all.60.parts, f32[2048,1024]{1,0:T(8,128)S(1)} %get-tuple-element.24.cross), custom_call_target="tpu_custom_call" | custom-call | tf_op jit(solution)/shard_map/pallas_call | solution.py:220
  100.3 9.2 %all_to_all.61.parts.gen_parts = f32[8,8,128]{2,1,0:T(8,128)S(1)} all-to-all(f32[8,8,128]{2,1,0:T(8,128)S(1)} %shard_map.73), channel_id=1, replica_groups=mesh['gen'=32,'beam'=8] {'beam'}, dimensions={0} | all-to-all | bytes 65536 | tf_op jit(solution)/shard_map/all_to_all | solution.py:231
  109.6 2.0 %shard_map.74 = (f32[32,16,128]{2,1,0:T(8,128)S(1)}, f32[1024,2048]{1,0:T(8,128)S(1)}, f32[32,128]{1,0:T(8,128)S(1)}) custom-call(f32[8,128]{1,0:T(8,128)S(1)} %get-tuple-element.17.table, f32[8,8,128]{2,1,0:T(8,128)S(1)} %all_to_all.61.parts.gen_parts, f32[1024,2048]{1,0:T(8,128)S(1)} %get-tuple-element.23.cross), custom_call_target="tpu_custom_call" | custom-call | tf_op jit(solution)/shard_map/pallas_call | solution.py:220
  111.6 13.6 %all_to_all.62.parts = f32[32,16,128]{2,1,0:T(8,128)S(1)} all-to-all(f32[32,16,128]{2,1,0:T(8,128)S(1)} %get-tuple-element.25), channel_id=1, replica_groups=mesh['gen'=32,'beam'=8] {'gen'}, dimensions={0} | all-to-all | bytes 524288 | tf_op jit(solution)/shard_map/all_to_all | solution.py:231
  125.2 0.0 copy-done
  125.2 0.0 copy-done.1
  125.2 4.1 %shard_map.75 = (f32[8,128]{1,0:T(8,128)}, f32[16,128]{1,0:T(8,128)}, f32[256,128]{1,0:T(8,128)S(1)}) custom-call(f32[8,128]{1,0:T(8,128)S(1)} %get-tuple-element.17.table, f32[32,16,128]{2,1,0:T(8,128)S(1)} %all_to_all.62.parts, f32[8,8,128]{2,1,0:T(8,128)S(1)} %all_to_all.61.parts.gen_parts, f32[1024,2048]{1,0:T(8,128)S(1)} %get-tuple-element.26.kernel, ...), custom_call_target="tpu_custom_call" | custom-call | tf_op jit(solution)/shard_map/pallas_call | solution.py:220
  129.3 11.2 %all_to_all.63 = f32[32,8,128]{2,1,0:T(8,128)S(1)} all-to-all(f32[32,8,128]{2,1,0:T(8,128)S(1)} %bitcast.5), channel_id=1, replica_groups=mesh['gen'=32,'beam'=8] {'gen'}, dimensions={0} | all-to-all | bytes 262144 | tf_op jit(solution)/shard_map/all_to_all | solution.py:231
  140.5 9.2 %all_to_all.64 = f32[8,8,128]{2,1,0:T(8,128)S(1)} all-to-all(f32[8,8,128]{2,1,0:T(8,128)S(1)} %broadcast_in_dim.4), channel_id=1, replica_groups=mesh['gen'=32,'beam'=8] {'beam'}, dimensions={0} | all-to-all | bytes 65536 | tf_op jit(solution)/shard_map/all_to_all | solution.py:231
  149.8 12.4 %all_to_all.65 = f32[32,8,128]{2,1,0:T(8,128)S(1)} all-to-all(f32[32,8,128]{2,1,0:T(8,128)S(1)} %broadcast_in_dim.5), channel_id=1, replica_groups=mesh['gen'=32,'beam'=8] {'gen'}, dimensions={0} | all-to-all | bytes 262144 | tf_op jit(solution)/shard_map/all_to_all | solution.py:231
  162.2 0.7 copy.8
  (4 shorter events, 0.1 us)
Async XLA Ops:
  0.6 0.8 copy-start.2
  1.5 0.7 copy-start.3
  98.3 26.9 %copy-start = (bf16[2048,256]{1,0:T(8,128)(2,1)S(1)}, bf16[2048,256]{1,0:T(8,128)(2,1)}, u32[]{:S(2)}) copy-start(bf16[2048,256]{1,0:T(8,128)(2,1)} %beam_showers.1) | copy-start | bytes 3145732
  98.3 26.9 %copy-start.1 = (bf16[1024,256]{1,0:T(8,128)(2,1)S(1)}, bf16[1024,256]{1,0:T(8,128)(2,1)}, u32[]{:S(2)}) copy-start(bf16[1024,256]{1,0:T(8,128)(2,1)} %gen_showers.1) | copy-start | bytes 1572868

commit v5 on v4

--- a/solution.py
+++ b/solution.py
@@ -11,13 +11,13 @@
 SWEEPS = 4
 LOG2E = 1.4426950408889634
 BYTES = 16 * 1024 * 1024
-FIRST_BYTES = 53 * 1024 * 1024
 NT = (((1,), (1,)), ((), ()))
 F32 = jnp.float32
 BF16 = jnp.bfloat16
 WIDE = 256
 BLOCK = 64
-DEEP = 512
+DEEP = 1024
+LAST_WIDE = 512
 
 
 def of_sweep(table, sweep):
@@ -101,8 +101,8 @@
 
 
 def first_kernel(
-    eps_far, gen_far, beam_far, weight_far, out, gen_emb, beam_emb, table,
-    column, top_scr, sum_scr, cross, eps, gen_showers, beam_showers, weight, sems,
+    eps_far, gen_far, beam_far, weight_far, out, cross, gen_emb, beam_emb, table,
+    column, top_scr, sum_scr, eps, gen_showers, beam_showers, weight, sems,
 ):
     pairs = ((weight_far, weight), (beam_far, beam_showers), (gen_far, gen_showers), (eps_far, eps))
     copies = [pltpu.make_async_copy(src, dst, sems.at[i]) for i, (src, dst) in enumerate(pairs)]
@@ -156,7 +156,7 @@
     count = stats.shape[0] // 2
     factor = jnp.exp2((stats[:count, :] + beam_half) * scale - log_beam * LOG2E)
     col_mass = stats[count:, :] * factor
-    tiles = WIDE // 128
+    tiles = LAST_WIDE // 128
 
     def line(dense, n):
         return jnp.concatenate([dense[n * tiles + i : n * tiles + i + 1, :] for i in range(tiles)], axis=1)
@@ -172,8 +172,8 @@
         gen_pot[r : r + 1, :] = 2.0 * gen_half[r : r + 1, :] + square(turned)
 
     total = None
-    for n in range(kernel.shape[1] // WIDE):
-        at = slice(n * WIDE, (n + 1) * WIDE)
+    for n in range(kernel.shape[1] // LAST_WIDE):
+        at = slice(n * LAST_WIDE, (n + 1) * LAST_WIDE)
         mass = kernel[:, at] * line(factor, n)
         plan = mass.astype(BF16)
         sums = mass[:, :128]
@@ -212,8 +212,9 @@
 FAR = pl.BlockSpec(memory_space=pltpu.HBM)
 
 
-def call(kernel, operands, outs, scratch=(), far=(), sems=0, limit=BYTES):
+def call(kernel, operands, outs, scratch=(), far=(), sems=0):
     specs = [FAR if i in far else LOCAL for i in range(len(operands))]
+    operands = [pltpu.with_memory_space_constraint(a, pltpu.HBM) if i in far else a for i, a in enumerate(operands)]
     scratch = [pltpu.VMEM(*s) for s in scratch]
     if sems:
         scratch.append(pltpu.SemaphoreType.DMA((sems,)))
@@ -223,7 +224,7 @@
         in_specs=specs,
         out_specs=tuple(LOCAL for _ in outs),
         scratch_shapes=scratch,
-        compiler_params=pltpu.CompilerParams(vmem_limit_bytes=limit),
+        compiler_params=pltpu.CompilerParams(vmem_limit_bytes=BYTES),
     )(*operands)
 
 
@@ -241,16 +242,15 @@
     gen_out, beam_out = ((beams, r, 128), F32), ((gens, c, 128), F32)
     gen_scratch = [((columns, 128), F32), ((r, 128), F32), ((r, 128), F32)]
     beam_scratch = [((rows, 128), F32), ((c, 128), F32), ((c, 128), F32)]
-    gen_parts, gen_emb, beam_emb, table = call(
+    gen_parts, turned_cross, gen_emb, beam_emb, table = call(
         first_kernel,
         (eps_roster, gen_showers, beam_showers, embed_weight),
-        [gen_out, ((rows, width), BF16), ((columns, width), BF16), ((2 * SWEEPS, 128), F32)],
+        [gen_out, ((columns, rows), F32), ((rows, width), BF16), ((columns, width), BF16), ((2 * SWEEPS, 128), F32)],
         gen_scratch
-        + [((columns, rows), F32), (eps_roster.shape, F32)]
+        + [(eps_roster.shape, F32)]
         + [(a.shape, BF16) for a in (gen_showers, beam_showers, embed_weight)],
         far=(0, 1, 2, 3),
         sems=4,
-        limit=FIRST_BYTES,
     )
     gen_parts = swap(gen_parts, "beam")
     beam_parts, cross = call(
@@ -261,20 +261,12 @@
     )
     for sweep in range(1, SWEEPS):
         beam_parts = swap(beam_parts, "gen")
-        if sweep == 1:
-            gen_parts, turned_cross = call(
-                functools.partial(made_kernel, sweep - 1, sweep, log_gen),
-                (table, beam_parts, beam_emb, gen_emb),
-                [gen_out, ((columns, rows), F32)],
-                gen_scratch,
-            )
-        else:
-            (gen_parts,) = call(
-                functools.partial(pass_kernel, sweep - 1, sweep, log_gen),
-                (table, beam_parts, turned_cross),
-                [gen_out],
-                gen_scratch,
-            )
+        (gen_parts,) = call(
+            functools.partial(pass_kernel, sweep - 1, sweep, log_gen),
+            (table, beam_parts, turned_cross),
+            [gen_out],
+            gen_scratch,
+        )
         gen_parts = swap(gen_parts, "beam")
         if sweep < SWEEPS - 1:
             (beam_parts,) = call(

time: 163 us -> 161 us (0.988)
  no operation moved by 1% of the time
where the time goes in v5:
time: 161 us; the launch traced here: 160 us
  blocking collectives  135 us (84%)
  Pallas kernels  23.8 us (15%)
    all_to_all x11, blocking collectives, swap(): return lax.all_to_all(x, axis, split_axis=0, concat_axis=0, tiled=True)  135 us
    pallas_call x9, Pallas kernels, call(): pl.pallas_call(kernel, out_shape=tuple((jax.ShapeDtypeStruct(*o) for o in...  23.8 us

profile of v5, /device:TPU:1, one launch (start us, length us, event | category | flops | bytes accessed | tf_op | source)
XLA Modules:
  0.0 160.2 jit_solution(12877860329503256924)
XLA Ops:
  0.6 5.1 %shard_map.67 = (f32[8,8,128]{2,1,0:T(8,128)S(1)}, f32[2048,1024]{1,0:T(8,128)S(1)}, bf16[1024,128]{1,0:T(8,128)(2,1)S(1)}, bf16[2048,128]{1,0:T(8,128)(2,1)S(1)}, f32[8,128]{1,0:T(8,128)S(1)}) custom-call(f32[1,4]{1,0:T(1,128)} %bitcast.7, bf16[1024,256]{1,0:T(8,128)(2,1)} %gen_showers.1, bf16[2048,256]{1,0:T(8,128)(2,1)} %beam_showers.1, ...), custom_call_target="tpu_custom_call" | custom-call | tf_op jit(solution)/shard_map/pallas_call | solution.py:221
  5.8 15.7 %all_to_all.55.parts = f32[8,8,128]{2,1,0:T(8,128)S(1)} all-to-all(f32[8,8,128]{2,1,0:T(8,128)S(1)} %get-tuple-element.17), channel_id=1, replica_groups=mesh['gen'=32,'beam'=8] {'beam'}, dimensions={0} | all-to-all | bytes 65536 | tf_op jit(solution)/shard_map/all_to_all | solution.py:232
  21.5 2.7 %shard_map.68 = (f32[32,16,128]{2,1,0:T(8,128)S(1)}, f32[1024,2048]{1,0:T(8,128)S(1)}) custom-call(f32[8,128]{1,0:T(8,128)S(1)} %get-tuple-element.16.table, f32[8,8,128]{2,1,0:T(8,128)S(1)} %all_to_all.55.parts, bf16[1024,128]{1,0:T(8,128)(2,1)S(1)} %get-tuple-element.18.summed.gen_emb, bf16[2048,128]{1,0:T(8,128)(2,1)S(1)} %get-tuple-element.19.kept.beam_emb), custom_call_target="tpu_custom_call" | custom-call | tf_op jit(solution)/shard_map/pallas_call | solution.py:221
  24.2 17.9 %all_to_all.56.parts = f32[32,16,128]{2,1,0:T(8,128)S(1)} all-to-all(f32[32,16,128]{2,1,0:T(8,128)S(1)} %get-tuple-element.20), channel_id=1, replica_groups=mesh['gen'=32,'beam'=8] {'gen'}, dimensions={0} | all-to-all | bytes 524288 | tf_op jit(solution)/shard_map/all_to_all | solution.py:232
  42.1 2.0 %shard_map.69 = f32[8,8,128]{2,1,0:T(8,128)S(1)} custom-call(f32[8,128]{1,0:T(8,128)S(1)} %get-tuple-element.16.table, f32[32,16,128]{2,1,0:T(8,128)S(1)} %all_to_all.56.parts, f32[2048,1024]{1,0:T(8,128)S(1)} %get-tuple-element.21.cross), custom_call_target="tpu_custom_call" | custom-call | tf_op jit(solution)/shard_map/pallas_call | solution.py:221
  44.1 9.2 %all_to_all.57.parts = f32[8,8,128]{2,1,0:T(8,128)S(1)} all-to-all(f32[8,8,128]{2,1,0:T(8,128)S(1)} %shard_map.69), channel_id=1, replica_groups=mesh['gen'=32,'beam'=8] {'beam'}, dimensions={0} | all-to-all | bytes 65536 | tf_op jit(solution)/shard_map/all_to_all | solution.py:232
  53.3 2.0 %shard_map.70 = f32[32,16,128]{2,1,0:T(8,128)S(1)} custom-call(f32[8,128]{1,0:T(8,128)S(1)} %get-tuple-element.16.table, f32[8,8,128]{2,1,0:T(8,128)S(1)} %all_to_all.57.parts, f32[1024,2048]{1,0:T(8,128)S(1)} %get-tuple-element.22.cross), custom_call_target="tpu_custom_call" | custom-call | tf_op jit(solution)/shard_map/pallas_call | solution.py:221
  55.4 13.6 %all_to_all.58.parts = f32[32,16,128]{2,1,0:T(8,128)S(1)} all-to-all(f32[32,16,128]{2,1,0:T(8,128)S(1)} %shard_map.70), channel_id=1, replica_groups=mesh['gen'=32,'beam'=8] {'gen'}, dimensions={0} | all-to-all | bytes 524288 | tf_op jit(solution)/shard_map/all_to_all | solution.py:232
  69.0 2.0 %shard_map.71 = f32[8,8,128]{2,1,0:T(8,128)S(1)} custom-call(f32[8,128]{1,0:T(8,128)S(1)} %get-tuple-element.16.table, f32[32,16,128]{2,1,0:T(8,128)S(1)} %all_to_all.58.parts, f32[2048,1024]{1,0:T(8,128)S(1)} %get-tuple-element.21.cross), custom_call_target="tpu_custom_call" | custom-call | tf_op jit(solution)/shard_map/pallas_call | solution.py:221
  71.0 9.2 %all_to_all.59.parts = f32[8,8,128]{2,1,0:T(8,128)S(1)} all-to-all(f32[8,8,128]{2,1,0:T(8,128)S(1)} %shard_map.71), channel_id=1, replica_groups=mesh['gen'=32,'beam'=8] {'beam'}, dimensions={0} | all-to-all | bytes 65536 | tf_op jit(solution)/shard_map/all_to_all | solution.py:232
  80.3 2.0 %shard_map.72 = f32[32,16,128]{2,1,0:T(8,128)S(1)} custom-call(f32[8,128]{1,0:T(8,128)S(1)} %get-tuple-element.16.table, f32[8,8,128]{2,1,0:T(8,128)S(1)} %all_to_all.59.parts, f32[1024,2048]{1,0:T(8,128)S(1)} %get-tuple-element.22.cross), custom_call_target="tpu_custom_call" | custom-call | tf_op jit(solution)/shard_map/pallas_call | solution.py:221
  82.3 13.6 %all_to_all.60.parts = f32[32,16,128]{2,1,0:T(8,128)S(1)} all-to-all(f32[32,16,128]{2,1,0:T(8,128)S(1)} %shard_map.72), channel_id=1, replica_groups=mesh['gen'=32,'beam'=8] {'gen'}, dimensions={0} | all-to-all | bytes 524288 | tf_op jit(solution)/shard_map/all_to_all | solution.py:232
  95.9 0.0 copy-start
  95.9 0.0 copy-start.1
  95.9 0.0 copy-start.2
  95.9 2.0 %shard_map.73 = f32[8,8,128]{2,1,0:T(8,128)S(1)} custom-call(f32[8,128]{1,0:T(8,128)S(1)} %get-tuple-element.16.table, f32[32,16,128]{2,1,0:T(8,128)S(1)} %all_to_all.60.parts, f32[2048,1024]{1,0:T(8,128)S(1)} %get-tuple-element.21.cross), custom_call_target="tpu_custom_call" | custom-call | tf_op jit(solution)/shard_map/pallas_call | solution.py:221
  98.0 9.2 %all_to_all.61.parts.gen_parts = f32[8,8,128]{2,1,0:T(8,128)S(1)} all-to-all(f32[8,8,128]{2,1,0:T(8,128)S(1)} %shard_map.73), channel_id=1, replica_groups=mesh['gen'=32,'beam'=8] {'beam'}, dimensions={0} | all-to-all | bytes 65536 | tf_op jit(solution)/shard_map/all_to_all | solution.py:232
  107.2 2.0 %shard_map.74 = (f32[32,16,128]{2,1,0:T(8,128)S(1)}, f32[1024,2048]{1,0:T(8,128)S(1)}, f32[32,128]{1,0:T(8,128)S(1)}) custom-call(f32[8,128]{1,0:T(8,128)S(1)} %get-tuple-element.16.table, f32[8,8,128]{2,1,0:T(8,128)S(1)} %all_to_all.61.parts.gen_parts, f32[1024,2048]{1,0:T(8,128)S(1)} %get-tuple-element.22.cross), custom_call_target="tpu_custom_call" | custom-call | tf_op jit(solution)/shard_map/pallas_call | solution.py:221
  109.2 13.6 %all_to_all.62.parts = f32[32,16,128]{2,1,0:T(8,128)S(1)} all-to-all(f32[32,16,128]{2,1,0:T(8,128)S(1)} %get-tuple-element.23), channel_id=1, replica_groups=mesh['gen'=32,'beam'=8] {'gen'}, dimensions={0} | all-to-all | bytes 524288 | tf_op jit(solution)/shard_map/all_to_all | solution.py:232
  122.9 0.0 copy-done
  122.9 0.0 copy-done.1
  122.9 0.0 copy-done.2
  122.9 3.7 %shard_map.75 = (f32[8,128]{1,0:T(8,128)}, f32[16,128]{1,0:T(8,128)}, f32[256,128]{1,0:T(8,128)S(1)}) custom-call(f32[8,128]{1,0:T(8,128)S(1)} %get-tuple-element.16.table, f32[32,16,128]{2,1,0:T(8,128)S(1)} %all_to_all.62.parts, f32[8,8,128]{2,1,0:T(8,128)S(1)} %all_to_all.61.parts.gen_parts, f32[1024,2048]{1,0:T(8,128)S(1)} %get-tuple-element.24.kernel, ...), custom_call_target="tpu_custom_call" | custom-call | tf_op jit(solution)/shard_map/pallas_call | solution.py:221
  126.6 11.2 %all_to_all.63 = f32[32,8,128]{2,1,0:T(8,128)S(1)} all-to-all(f32[32,8,128]{2,1,0:T(8,128)S(1)} %bitcast.5), channel_id=1, replica_groups=mesh['gen'=32,'beam'=8] {'gen'}, dimensions={0} | all-to-all | bytes 262144 | tf_op jit(solution)/shard_map/all_to_all | solution.py:232
  137.8 9.2 %all_to_all.64 = f32[8,8,128]{2,1,0:T(8,128)S(1)} all-to-all(f32[8,8,128]{2,1,0:T(8,128)S(1)} %broadcast_in_dim.4), channel_id=1, replica_groups=mesh['gen'=32,'beam'=8] {'beam'}, dimensions={0} | all-to-all | bytes 65536 | tf_op jit(solution)/shard_map/all_to_all | solution.py:232
  147.1 12.4 %all_to_all.65 = f32[32,8,128]{2,1,0:T(8,128)S(1)} all-to-all(f32[32,8,128]{2,1,0:T(8,128)S(1)} %broadcast_in_dim.5), channel_id=1, replica_groups=mesh['gen'=32,'beam'=8] {'gen'}, dimensions={0} | all-to-all | bytes 262144 | tf_op jit(solution)/shard_map/all_to_all | solution.py:232
  159.5 0.7 copy.8
  (4 shorter events, 0.1 us)
Async XLA Ops:
  95.9 26.9 %copy-start = (bf16[2048,256]{1,0:T(8,128)(2,1)S(1)}, bf16[2048,256]{1,0:T(8,128)(2,1)}, u32[]{:S(2)}) copy-start(bf16[2048,256]{1,0:T(8,128)(2,1)} %beam_showers.1) | copy-start | bytes 3145732
  95.9 26.9 %copy-start.1 = (bf16[1024,256]{1,0:T(8,128)(2,1)S(1)}, bf16[1024,256]{1,0:T(8,128)(2,1)}, u32[]{:S(2)}) copy-start(bf16[1024,256]{1,0:T(8,128)(2,1)} %gen_showers.1) | copy-start | bytes 1572868
  95.9 26.9 %copy-start.2 = (bf16[256,128]{1,0:T(8,128)(2,1)S(1)}, bf16[256,128]{1,0:T(8,128)(2,1)}, u32[]{:S(2)}) copy-start(bf16[256,128]{1,0:T(8,128)(2,1)} %weight.1) | copy-start | bytes 196612

commit v6 on v5

--- a/solution.py
+++ b/solution.py
@@ -110,13 +110,13 @@
         copy.start()
     copies[0].wait()
     copies[1].wait()
+    copies[2].wait()
+    copies[3].wait()
     beam = embed(beam_showers, weight).astype(BF16)
     beam_emb[...] = beam
     beam = beam.astype(F32)
     column[...] = jnp.broadcast_to(-0.5 * jnp.sum(beam * beam, axis=1, keepdims=True), column.shape)
-    copies[2].wait()
     gen_emb[...] = embed(gen_showers, weight).astype(BF16)
-    copies[3].wait()
     tabled(eps, table)
     partial_lse(cross, column, table, 0, top_scr, sum_scr, out, (beam_emb, gen_emb))
 

time: 161 us -> 160 us (level)
  no operation moved by 1% of the time
where the time goes in v6:
time: 160 us
  blocking collectives  135 us (84%)
  Pallas kernels  23.4 us (15%)
    all_to_all x11, blocking collectives, swap(): return lax.all_to_all(x, axis, split_axis=0, concat_axis=0, tiled=True)  135 us
    pallas_call x9, Pallas kernels, call(): pl.pallas_call(kernel, out_shape=tuple((jax.ShapeDtypeStruct(*o) for o in...  23.4 us

profile of v6, /device:TPU:1, one launch (start us, length us, event | category | flops | bytes accessed | tf_op | source)
XLA Modules:
  0.0 159.8 jit_solution(16130880020641467478)
XLA Ops:
  0.6 4.7 %shard_map.67 = (f32[8,8,128]{2,1,0:T(8,128)S(1)}, f32[2048,1024]{1,0:T(8,128)S(1)}, bf16[1024,128]{1,0:T(8,128)(2,1)S(1)}, bf16[2048,128]{1,0:T(8,128)(2,1)S(1)}, f32[8,128]{1,0:T(8,128)S(1)}) custom-call(f32[1,4]{1,0:T(1,128)} %bitcast.7, bf16[1024,256]{1,0:T(8,128)(2,1)} %gen_showers.1, bf16[2048,256]{1,0:T(8,128)(2,1)} %beam_showers.1, ...), custom_call_target="tpu_custom_call" | custom-call | tf_op jit(solution)/shard_map/pallas_call | solution.py:221
  5.3 15.7 %all_to_all.55.parts = f32[8,8,128]{2,1,0:T(8,128)S(1)} all-to-all(f32[8,8,128]{2,1,0:T(8,128)S(1)} %get-tuple-element.17), channel_id=1, replica_groups=mesh['gen'=32,'beam'=8] {'beam'}, dimensions={0} | all-to-all | bytes 65536 | tf_op jit(solution)/shard_map/all_to_all | solution.py:232
  21.0 2.7 %shard_map.68 = (f32[32,16,128]{2,1,0:T(8,128)S(1)}, f32[1024,2048]{1,0:T(8,128)S(1)}) custom-call(f32[8,128]{1,0:T(8,128)S(1)} %get-tuple-element.16.table, f32[8,8,128]{2,1,0:T(8,128)S(1)} %all_to_all.55.parts, bf16[1024,128]{1,0:T(8,128)(2,1)S(1)} %get-tuple-element.18.summed.gen_emb, bf16[2048,128]{1,0:T(8,128)(2,1)S(1)} %get-tuple-element.19.kept.beam_emb), custom_call_target="tpu_custom_call" | custom-call | tf_op jit(solution)/shard_map/pallas_call | solution.py:221
  23.8 17.9 %all_to_all.56.parts = f32[32,16,128]{2,1,0:T(8,128)S(1)} all-to-all(f32[32,16,128]{2,1,0:T(8,128)S(1)} %get-tuple-element.20), channel_id=1, replica_groups=mesh['gen'=32,'beam'=8] {'gen'}, dimensions={0} | all-to-all | bytes 524288 | tf_op jit(solution)/shard_map/all_to_all | solution.py:232
  41.7 2.0 %shard_map.69 = f32[8,8,128]{2,1,0:T(8,128)S(1)} custom-call(f32[8,128]{1,0:T(8,128)S(1)} %get-tuple-element.16.table, f32[32,16,128]{2,1,0:T(8,128)S(1)} %all_to_all.56.parts, f32[2048,1024]{1,0:T(8,128)S(1)} %get-tuple-element.21.cross), custom_call_target="tpu_custom_call" | custom-call | tf_op jit(solution)/shard_map/pallas_call | solution.py:221
  43.7 9.2 %all_to_all.57.parts = f32[8,8,128]{2,1,0:T(8,128)S(1)} all-to-all(f32[8,8,128]{2,1,0:T(8,128)S(1)} %shard_map.69), channel_id=1, replica_groups=mesh['gen'=32,'beam'=8] {'beam'}, dimensions={0} | all-to-all | bytes 65536 | tf_op jit(solution)/shard_map/all_to_all | solution.py:232
  52.9 2.0 %shard_map.70 = f32[32,16,128]{2,1,0:T(8,128)S(1)} custom-call(f32[8,128]{1,0:T(8,128)S(1)} %get-tuple-element.16.table, f32[8,8,128]{2,1,0:T(8,128)S(1)} %all_to_all.57.parts, f32[1024,2048]{1,0:T(8,128)S(1)} %get-tuple-element.22.cross), custom_call_target="tpu_custom_call" | custom-call | tf_op jit(solution)/shard_map/pallas_call | solution.py:221
  55.0 13.6 %all_to_all.58.parts = f32[32,16,128]{2,1,0:T(8,128)S(1)} all-to-all(f32[32,16,128]{2,1,0:T(8,128)S(1)} %shard_map.70), channel_id=1, replica_groups=mesh['gen'=32,'beam'=8] {'gen'}, dimensions={0} | all-to-all | bytes 524288 | tf_op jit(solution)/shard_map/all_to_all | solution.py:232
  68.6 2.0 %shard_map.71 = f32[8,8,128]{2,1,0:T(8,128)S(1)} custom-call(f32[8,128]{1,0:T(8,128)S(1)} %get-tuple-element.16.table, f32[32,16,128]{2,1,0:T(8,128)S(1)} %all_to_all.58.parts, f32[2048,1024]{1,0:T(8,128)S(1)} %get-tuple-element.21.cross), custom_call_target="tpu_custom_call" | custom-call | tf_op jit(solution)/shard_map/pallas_call | solution.py:221
  70.6 9.2 %all_to_all.59.parts = f32[8,8,128]{2,1,0:T(8,128)S(1)} all-to-all(f32[8,8,128]{2,1,0:T(8,128)S(1)} %shard_map.71), channel_id=1, replica_groups=mesh['gen'=32,'beam'=8] {'beam'}, dimensions={0} | all-to-all | bytes 65536 | tf_op jit(solution)/shard_map/all_to_all | solution.py:232
  79.9 2.0 %shard_map.72 = f32[32,16,128]{2,1,0:T(8,128)S(1)} custom-call(f32[8,128]{1,0:T(8,128)S(1)} %get-tuple-element.16.table, f32[8,8,128]{2,1,0:T(8,128)S(1)} %all_to_all.59.parts, f32[1024,2048]{1,0:T(8,128)S(1)} %get-tuple-element.22.cross), custom_call_target="tpu_custom_call" | custom-call | tf_op jit(solution)/shard_map/pallas_call | solution.py:221
  81.9 13.6 %all_to_all.60.parts = f32[32,16,128]{2,1,0:T(8,128)S(1)} all-to-all(f32[32,16,128]{2,1,0:T(8,128)S(1)} %shard_map.72), channel_id=1, replica_groups=mesh['gen'=32,'beam'=8] {'gen'}, dimensions={0} | all-to-all | bytes 524288 | tf_op jit(solution)/shard_map/all_to_all | solution.py:232
  95.5 0.0 copy-start
  95.5 0.0 copy-start.1
  95.5 0.0 copy-start.2
  95.5 2.0 %shard_map.73 = f32[8,8,128]{2,1,0:T(8,128)S(1)} custom-call(f32[8,128]{1,0:T(8,128)S(1)} %get-tuple-element.16.table, f32[32,16,128]{2,1,0:T(8,128)S(1)} %all_to_all.60.parts, f32[2048,1024]{1,0:T(8,128)S(1)} %get-tuple-element.21.cross), custom_call_target="tpu_custom_call" | custom-call | tf_op jit(solution)/shard_map/pallas_call | solution.py:221
  97.5 9.2 %all_to_all.61.parts.gen_parts = f32[8,8,128]{2,1,0:T(8,128)S(1)} all-to-all(f32[8,8,128]{2,1,0:T(8,128)S(1)} %shard_map.73), channel_id=1, replica_groups=mesh['gen'=32,'beam'=8] {'beam'}, dimensions={0} | all-to-all | bytes 65536 | tf_op jit(solution)/shard_map/all_to_all | solution.py:232
  106.8 2.0 %shard_map.74 = (f32[32,16,128]{2,1,0:T(8,128)S(1)}, f32[1024,2048]{1,0:T(8,128)S(1)}, f32[32,128]{1,0:T(8,128)S(1)}) custom-call(f32[8,128]{1,0:T(8,128)S(1)} %get-tuple-element.16.table, f32[8,8,128]{2,1,0:T(8,128)S(1)} %all_to_all.61.parts.gen_parts, f32[1024,2048]{1,0:T(8,128)S(1)} %get-tuple-element.22.cross), custom_call_target="tpu_custom_call" | custom-call | tf_op jit(solution)/shard_map/pallas_call | solution.py:221
  108.8 13.6 %all_to_all.62.parts = f32[32,16,128]{2,1,0:T(8,128)S(1)} all-to-all(f32[32,16,128]{2,1,0:T(8,128)S(1)} %get-tuple-element.23), channel_id=1, replica_groups=mesh['gen'=32,'beam'=8] {'gen'}, dimensions={0} | all-to-all | bytes 524288 | tf_op jit(solution)/shard_map/all_to_all | solution.py:232
  122.4 0.0 copy-done
  122.4 0.0 copy-done.1
  122.5 0.0 copy-done.2
  122.5 3.7 %shard_map.75 = (f32[8,128]{1,0:T(8,128)}, f32[16,128]{1,0:T(8,128)}, f32[256,128]{1,0:T(8,128)S(1)}) custom-call(f32[8,128]{1,0:T(8,128)S(1)} %get-tuple-element.16.table, f32[32,16,128]{2,1,0:T(8,128)S(1)} %all_to_all.62.parts, f32[8,8,128]{2,1,0:T(8,128)S(1)} %all_to_all.61.parts.gen_parts, f32[1024,2048]{1,0:T(8,128)S(1)} %get-tuple-element.24.kernel, ...), custom_call_target="tpu_custom_call" | custom-call | tf_op jit(solution)/shard_map/pallas_call | solution.py:221
  126.2 11.2 %all_to_all.63 = f32[32,8,128]{2,1,0:T(8,128)S(1)} all-to-all(f32[32,8,128]{2,1,0:T(8,128)S(1)} %bitcast.5), channel_id=1, replica_groups=mesh['gen'=32,'beam'=8] {'gen'}, dimensions={0} | all-to-all | bytes 262144 | tf_op jit(solution)/shard_map/all_to_all | solution.py:232
  137.4 9.2 %all_to_all.64 = f32[8,8,128]{2,1,0:T(8,128)S(1)} all-to-all(f32[8,8,128]{2,1,0:T(8,128)S(1)} %broadcast_in_dim.4), channel_id=1, replica_groups=mesh['gen'=32,'beam'=8] {'beam'}, dimensions={0} | all-to-all | bytes 65536 | tf_op jit(solution)/shard_map/all_to_all | solution.py:232
  146.7 12.4 %all_to_all.65 = f32[32,8,128]{2,1,0:T(8,128)S(1)} all-to-all(f32[32,8,128]{2,1,0:T(8,128)S(1)} %broadcast_in_dim.5), channel_id=1, replica_groups=mesh['gen'=32,'beam'=8] {'gen'}, dimensions={0} | all-to-all | bytes 262144 | tf_op jit(solution)/shard_map/all_to_all | solution.py:232
  159.1 0.7 copy.8
  (4 shorter events, 0.1 us)
Async XLA Ops:
  95.5 26.9 %copy-start = (bf16[2048,256]{1,0:T(8,128)(2,1)S(1)}, bf16[2048,256]{1,0:T(8,128)(2,1)}, u32[]{:S(2)}) copy-start(bf16[2048,256]{1,0:T(8,128)(2,1)} %beam_showers.1) | copy-start | bytes 3145732
  95.5 26.9 %copy-start.1 = (bf16[1024,256]{1,0:T(8,128)(2,1)S(1)}, bf16[1024,256]{1,0:T(8,128)(2,1)}, u32[]{:S(2)}) copy-start(bf16[1024,256]{1,0:T(8,128)(2,1)} %gen_showers.1) | copy-start | bytes 1572868
  95.5 26.9 %copy-start.2 = (bf16[256,128]{1,0:T(8,128)(2,1)S(1)}, bf16[256,128]{1,0:T(8,128)(2,1)}, u32[]{:S(2)}) copy-start(bf16[256,128]{1,0:T(8,128)(2,1)} %weight.1) | copy-start | bytes 196612

commit v7 on v6

--- a/solution.py
+++ b/solution.py
@@ -16,7 +16,7 @@
 BF16 = jnp.bfloat16
 WIDE = 256
 BLOCK = 64
-DEEP = 1024
+DEEP = 2048
 LAST_WIDE = 512
 
 
@@ -50,7 +50,7 @@
 
 def partial_lse(cross, column, table, sweep, top_scr, sum_scr, out, factors=None, kernel=None):
     rows, lanes = cross.shape
-    count, tiles = lanes // WIDE, WIDE // 128
+    count, tiles, deep = lanes // WIDE, WIDE // 128, min(DEEP, rows)
     e, scale = of_sweep(table, sweep)
     wide_scale = jnp.concatenate([scale] * tiles, axis=1)
 
@@ -74,10 +74,10 @@
                 if factors is None:
                     t = cross[at, new]
                 else:
-                    if r % DEEP == 0:
+                    if r % deep == 0:
                         summed, kept = factors
-                        made = lax.dot_general(summed[r : r + DEEP, :], kept[new, :], NT, preferred_element_type=F32)
-                    t = made[r % DEEP : r % DEEP + BLOCK]
+                        made = lax.dot_general(summed[r : r + deep, :], kept[new, :], NT, preferred_element_type=F32)
+                    t = made[r % deep : r % deep + BLOCK]
                     cross[at, new] = t
                 t = fold(t + lift(r), jnp.max)
                 top = t if top is None else jnp.maximum(top, t)

time: 160 us -> 160 us (level)
  no operation moved by 1% of the time
where the time goes in v7:
time: 160 us
  blocking collectives  135 us (84%)
  Pallas kernels  23.3 us (15%)
    all_to_all x11, blocking collectives, swap(): return lax.all_to_all(x, axis, split_axis=0, concat_axis=0, tiled=True)  135 us
    pallas_call x9, Pallas kernels, call(): pl.pallas_call(kernel, out_shape=tuple((jax.ShapeDtypeStruct(*o) for o in...  23.3 us

profile of v7, /device:TPU:1, one launch (start us, length us, event | category | flops | bytes accessed | tf_op | source)
XLA Modules:
  0.0 159.7 jit_solution(15768223823392959998)
XLA Ops:
  0.6 4.6 %shard_map.67 = (f32[8,8,128]{2,1,0:T(8,128)S(1)}, f32[2048,1024]{1,0:T(8,128)S(1)}, bf16[1024,128]{1,0:T(8,128)(2,1)S(1)}, bf16[2048,128]{1,0:T(8,128)(2,1)S(1)}, f32[8,128]{1,0:T(8,128)S(1)}) custom-call(f32[1,4]{1,0:T(1,128)} %bitcast.7, bf16[1024,256]{1,0:T(8,128)(2,1)} %gen_showers.1, bf16[2048,256]{1,0:T(8,128)(2,1)} %beam_showers.1, ...), custom_call_target="tpu_custom_call" | custom-call | tf_op jit(solution)/shard_map/pallas_call | solution.py:221
  5.3 15.7 %all_to_all.55.parts = f32[8,8,128]{2,1,0:T(8,128)S(1)} all-to-all(f32[8,8,128]{2,1,0:T(8,128)S(1)} %get-tuple-element.17), channel_id=1, replica_groups=mesh['gen'=32,'beam'=8] {'beam'}, dimensions={0} | all-to-all | bytes 65536 | tf_op jit(solution)/shard_map/all_to_all | solution.py:232
  21.0 2.7 %shard_map.68 = (f32[32,16,128]{2,1,0:T(8,128)S(1)}, f32[1024,2048]{1,0:T(8,128)S(1)}) custom-call(f32[8,128]{1,0:T(8,128)S(1)} %get-tuple-element.16.table, f32[8,8,128]{2,1,0:T(8,128)S(1)} %all_to_all.55.parts, bf16[1024,128]{1,0:T(8,128)(2,1)S(1)} %get-tuple-element.18.summed.gen_emb, bf16[2048,128]{1,0:T(8,128)(2,1)S(1)} %get-tuple-element.19.kept.beam_emb), custom_call_target="tpu_custom_call" | custom-call | tf_op jit(solution)/shard_map/pallas_call | solution.py:221
  23.7 17.9 %all_to_all.56.parts = f32[32,16,128]{2,1,0:T(8,128)S(1)} all-to-all(f32[32,16,128]{2,1,0:T(8,128)S(1)} %get-tuple-element.20), channel_id=1, replica_groups=mesh['gen'=32,'beam'=8] {'gen'}, dimensions={0} | all-to-all | bytes 524288 | tf_op jit(solution)/shard_map/all_to_all | solution.py:232
  41.6 2.0 %shard_map.69 = f32[8,8,128]{2,1,0:T(8,128)S(1)} custom-call(f32[8,128]{1,0:T(8,128)S(1)} %get-tuple-element.16.table, f32[32,16,128]{2,1,0:T(8,128)S(1)} %all_to_all.56.parts, f32[2048,1024]{1,0:T(8,128)S(1)} %get-tuple-element.21.cross), custom_call_target="tpu_custom_call" | custom-call | tf_op jit(solution)/shard_map/pallas_call | solution.py:221
  43.6 9.2 %all_to_all.57.parts = f32[8,8,128]{2,1,0:T(8,128)S(1)} all-to-all(f32[8,8,128]{2,1,0:T(8,128)S(1)} %shard_map.69), channel_id=1, replica_groups=mesh['gen'=32,'beam'=8] {'beam'}, dimensions={0} | all-to-all | bytes 65536 | tf_op jit(solution)/shard_map/all_to_all | solution.py:232
  52.9 2.0 %shard_map.70 = f32[32,16,128]{2,1,0:T(8,128)S(1)} custom-call(f32[8,128]{1,0:T(8,128)S(1)} %get-tuple-element.16.table, f32[8,8,128]{2,1,0:T(8,128)S(1)} %all_to_all.57.parts, f32[1024,2048]{1,0:T(8,128)S(1)} %get-tuple-element.22.cross), custom_call_target="tpu_custom_call" | custom-call | tf_op jit(solution)/shard_map/pallas_call | solution.py:221
  54.9 13.6 %all_to_all.58.parts = f32[32,16,128]{2,1,0:T(8,128)S(1)} all-to-all(f32[32,16,128]{2,1,0:T(8,128)S(1)} %shard_map.70), channel_id=1, replica_groups=mesh['gen'=32,'beam'=8] {'gen'}, dimensions={0} | all-to-all | bytes 524288 | tf_op jit(solution)/shard_map/all_to_all | solution.py:232
  68.5 2.0 %shard_map.71 = f32[8,8,128]{2,1,0:T(8,128)S(1)} custom-call(f32[8,128]{1,0:T(8,128)S(1)} %get-tuple-element.16.table, f32[32,16,128]{2,1,0:T(8,128)S(1)} %all_to_all.58.parts, f32[2048,1024]{1,0:T(8,128)S(1)} %get-tuple-element.21.cross), custom_call_target="tpu_custom_call" | custom-call | tf_op jit(solution)/shard_map/pallas_call | solution.py:221
  70.6 9.2 %all_to_all.59.parts = f32[8,8,128]{2,1,0:T(8,128)S(1)} all-to-all(f32[8,8,128]{2,1,0:T(8,128)S(1)} %shard_map.71), channel_id=1, replica_groups=mesh['gen'=32,'beam'=8] {'beam'}, dimensions={0} | all-to-all | bytes 65536 | tf_op jit(solution)/shard_map/all_to_all | solution.py:232
  79.8 2.0 %shard_map.72 = f32[32,16,128]{2,1,0:T(8,128)S(1)} custom-call(f32[8,128]{1,0:T(8,128)S(1)} %get-tuple-element.16.table, f32[8,8,128]{2,1,0:T(8,128)S(1)} %all_to_all.59.parts, f32[1024,2048]{1,0:T(8,128)S(1)} %get-tuple-element.22.cross), custom_call_target="tpu_custom_call" | custom-call | tf_op jit(solution)/shard_map/pallas_call | solution.py:221
  81.9 13.6 %all_to_all.60.parts = f32[32,16,128]{2,1,0:T(8,128)S(1)} all-to-all(f32[32,16,128]{2,1,0:T(8,128)S(1)} %shard_map.72), channel_id=1, replica_groups=mesh['gen'=32,'beam'=8] {'gen'}, dimensions={0} | all-to-all | bytes 524288 | tf_op jit(solution)/shard_map/all_to_all | solution.py:232
  95.5 0.0 copy-start
  95.5 0.0 copy-start.1
  95.5 0.0 copy-start.2
  95.5 2.0 %shard_map.73 = f32[8,8,128]{2,1,0:T(8,128)S(1)} custom-call(f32[8,128]{1,0:T(8,128)S(1)} %get-tuple-element.16.table, f32[32,16,128]{2,1,0:T(8,128)S(1)} %all_to_all.60.parts, f32[2048,1024]{1,0:T(8,128)S(1)} %get-tuple-element.21.cross), custom_call_target="tpu_custom_call" | custom-call | tf_op jit(solution)/shard_map/pallas_call | solution.py:221
  97.5 9.2 %all_to_all.61.parts.gen_parts = f32[8,8,128]{2,1,0:T(8,128)S(1)} all-to-all(f32[8,8,128]{2,1,0:T(8,128)S(1)} %shard_map.73), channel_id=1, replica_groups=mesh['gen'=32,'beam'=8] {'beam'}, dimensions={0} | all-to-all | bytes 65536 | tf_op jit(solution)/shard_map/all_to_all | solution.py:232
  106.7 2.0 %shard_map.74 = (f32[32,16,128]{2,1,0:T(8,128)S(1)}, f32[1024,2048]{1,0:T(8,128)S(1)}, f32[32,128]{1,0:T(8,128)S(1)}) custom-call(f32[8,128]{1,0:T(8,128)S(1)} %get-tuple-element.16.table, f32[8,8,128]{2,1,0:T(8,128)S(1)} %all_to_all.61.parts.gen_parts, f32[1024,2048]{1,0:T(8,128)S(1)} %get-tuple-element.22.cross), custom_call_target="tpu_custom_call" | custom-call | tf_op jit(solution)/shard_map/pallas_call | solution.py:221
  108.8 13.6 %all_to_all.62.parts = f32[32,16,128]{2,1,0:T(8,128)S(1)} all-to-all(f32[32,16,128]{2,1,0:T(8,128)S(1)} %get-tuple-element.23), channel_id=1, replica_groups=mesh['gen'=32,'beam'=8] {'gen'}, dimensions={0} | all-to-all | bytes 524288 | tf_op jit(solution)/shard_map/all_to_all | solution.py:232
  122.4 0.0 copy-done
  122.4 0.0 copy-done.1
  122.4 0.0 copy-done.2
  122.4 3.7 %shard_map.75 = (f32[8,128]{1,0:T(8,128)}, f32[16,128]{1,0:T(8,128)}, f32[256,128]{1,0:T(8,128)S(1)}) custom-call(f32[8,128]{1,0:T(8,128)S(1)} %get-tuple-element.16.table, f32[32,16,128]{2,1,0:T(8,128)S(1)} %all_to_all.62.parts, f32[8,8,128]{2,1,0:T(8,128)S(1)} %all_to_all.61.parts.gen_parts, f32[1024,2048]{1,0:T(8,128)S(1)} %get-tuple-element.24.kernel, ...), custom_call_target="tpu_custom_call" | custom-call | tf_op jit(solution)/shard_map/pallas_call | solution.py:221
  126.1 11.2 %all_to_all.63 = f32[32,8,128]{2,1,0:T(8,128)S(1)} all-to-all(f32[32,8,128]{2,1,0:T(8,128)S(1)} %bitcast.5), channel_id=1, replica_groups=mesh['gen'=32,'beam'=8] {'gen'}, dimensions={0} | all-to-all | bytes 262144 | tf_op jit(solution)/shard_map/all_to_all | solution.py:232
  137.4 9.2 %all_to_all.64 = f32[8,8,128]{2,1,0:T(8,128)S(1)} all-to-all(f32[8,8,128]{2,1,0:T(8,128)S(1)} %broadcast_in_dim.4), channel_id=1, replica_groups=mesh['gen'=32,'beam'=8] {'beam'}, dimensions={0} | all-to-all | bytes 65536 | tf_op jit(solution)/shard_map/all_to_all | solution.py:232
  146.6 12.4 %all_to_all.65 = f32[32,8,128]{2,1,0:T(8,128)S(1)} all-to-all(f32[32,8,128]{2,1,0:T(8,128)S(1)} %broadcast_in_dim.5), channel_id=1, replica_groups=mesh['gen'=32,'beam'=8] {'gen'}, dimensions={0} | all-to-all | bytes 262144 | tf_op jit(solution)/shard_map/all_to_all | solution.py:232
  159.1 0.7 copy.8
  (4 shorter events, 0.1 us)
Async XLA Ops:
  95.5 26.9 %copy-start = (bf16[2048,256]{1,0:T(8,128)(2,1)S(1)}, bf16[2048,256]{1,0:T(8,128)(2,1)}, u32[]{:S(2)}) copy-start(bf16[2048,256]{1,0:T(8,128)(2,1)} %beam_showers.1) | copy-start | bytes 3145732
  95.5 26.9 %copy-start.1 = (bf16[1024,256]{1,0:T(8,128)(2,1)S(1)}, bf16[1024,256]{1,0:T(8,128)(2,1)}, u32[]{:S(2)}) copy-start(bf16[1024,256]{1,0:T(8,128)(2,1)} %gen_showers.1) | copy-start | bytes 1572868
  95.5 26.9 %copy-start.2 = (bf16[256,128]{1,0:T(8,128)(2,1)S(1)}, bf16[256,128]{1,0:T(8,128)(2,1)}, u32[]{:S(2)}) copy-start(bf16[256,128]{1,0:T(8,128)(2,1)} %weight.1) | copy-start | bytes 196612
